TPU v7x, 128 devices: a whole 4x4x4 slice. The times are simulated.
128 devices in a mesh: tm: 16 (over x, y), space: 8 (over z, core).
Axes of the slice: x: 4, y: 4, z: 4, core: 2. Of those that a mesh axis runs over, the one named last changes fastest.
Arguments:
- forcing: float32 [256, 65536], P('tm', 'space'), may hold values from -6 to 6
- op_main: bfloat16 [1024, 64, 448], P('space'), may hold values from -0.1205 to 2.61
- op_mass: bfloat16 [1024, 64, 448], P('space'), may hold values from -0.0401 to 1.045
- jacobi_inv: bfloat16 [1024, 64, 64], P('space'), may hold values from -0.0301 to 0.635
Outputs:
- spec_real: float32 [256, 65536], P('tm', 'space')
- spec_imag: float32 [256, 65536], P('tm', 'space')
- time_field: float32 [256, 65536], P('tm', 'space')
All inputs are finite; a program needn't handle non-finite values.
Results may differ from a plain program's by a relative error of at most 0.0058.
Values may be sent and summed in bfloat16 or wider, within the bound.
No kernel may reach another device: no remote copies, remote signals or barrier semaphores. Data moves between devices by JAX's collectives and lax.ppermute only.
A program may use at most 128 MiB of HBM per device.

v0:
```python
import functools
import math

import jax
import jax.numpy as jnp
import ml_dtypes
import numpy as np
from jax import lax
from jax.experimental import pallas as pl
from jax.experimental.pallas import tpu as pltpu
from jax.sharding import PartitionSpec as P

LENGTH = 256
PARTS = 16
STEPS = LENGTH // PARTS
BS = 64
LAYER = 1024
ROW = 256
LAYERS = 8
SLAB = LAYERS * LAYER
BLOCKS = SLAB // BS
SLOTS = 7
COL = 128
OWN = 4 * COL
BOX = 12 * COL
CHUNK = 16

ALPHA = 0.25
LOG_STEP = math.log(ALPHA) / LENGTH
MODULUS = ALPHA ** (1.0 / LENGTH)

f32 = jnp.float32
bf16 = jnp.bfloat16


def box_of(part):
    return part // 4, part // 2 % 2, part % 2


def dft_table():
    freq = np.arange(LENGTH)[:, None]
    step = np.arange(LENGTH)[None, :]
    angle = 2.0 * np.pi * (freq * step % LENGTH) / LENGTH
    table = np.stack([np.cos(angle), -np.sin(angle)], 1) / math.sqrt(LENGTH)
    table = table.reshape(PARTS, STEPS, 2, LENGTH).transpose(0, 2, 1, 3)
    table = table.reshape(2 * LENGTH, LENGTH)
    high = table.astype(ml_dtypes.bfloat16)
    low = (table - high.astype(np.float64)).astype(ml_dtypes.bfloat16)
    return np.concatenate([high, high, low], axis=1)


def step_ids(part, count, width):
    return part * STEPS + lax.broadcasted_iota(jnp.int32, (count, width), 0)


def cost(flops, nbytes):
    return pl.CostEstimate(flops=flops, bytes_accessed=nbytes, transcendentals=0)


def dot(a, b):
    return jnp.dot(a, b, preferred_element_type=f32)


def pack_kernel(forcing, low_edge, high_edge, out):
    part = lax.axis_index("tm")
    ids = step_ids(part, STEPS, COL).astype(f32)
    scale = jnp.exp(ids * LOG_STEP)
    half = lax.broadcasted_iota(jnp.int32, (STEPS, COL), 1) < BS
    cols = {}

    def column(z, y, x):
        at = z * LAYER + y * ROW + x * COL
        if at not in cols:
            cols[at] = forcing[:, at : at + COL] * scale
        return cols[at]

    def put(dest, c, value):
        out[dest, :, c * COL : (c + 1) * COL] = value.astype(bf16)

    for dest in range(PARTS):
        zg, yg, xg = box_of(dest)
        for d in range(2):
            for e in range(2):
                put(dest, 2 * d + e, column(2 * zg + d, 2 * yg + e, xg))
            y = 2 * yg + d
            at = y * ROW + xg * COL
            if zg == 0:
                put(dest, 4 + d, low_edge[:, at : at + COL])
            else:
                put(dest, 4 + d, column(2 * zg - 1, y, xg))
            if zg == 3:
                put(dest, 6 + d, high_edge[:, at : at + COL])
            else:
                put(dest, 6 + d, column(2 * zg + 2, y, xg))
            z = 2 * zg + d
            put(dest, 8 + d, column(z, 2 - yg, xg))
            first = column(z, 2 * yg, 1 - xg)
            second = column(z, 2 * yg + 1, 1 - xg)
            if xg == 0:
                pair = jnp.where(half, first, pltpu.roll(second, BS, 1))
            else:
                pair = jnp.where(half, pltpu.roll(first, BS, 1), second)
            put(dest, 10 + d, pair)


def pack(forcing, low_edge, high_edge):
    return pl.pallas_call(
        pack_kernel,
        out_shape=jax.ShapeDtypeStruct((PARTS, STEPS, BOX), bf16),
        name="pack",
        cost_estimate=cost(10**6, 2 * 10**6),
    )(forcing, low_edge, high_edge)


def selector(blocks, width):
    block = lax.broadcasted_iota(jnp.int32, (BLOCKS, width), 0)
    lane = lax.broadcasted_iota(jnp.int32, (BLOCKS, width), 1)
    hit = block == blocks
    pieces = [
        jnp.where(hit & (lane % CHUNK == o), 1.0, 0.0).astype(bf16) for o in range(CHUNK)
    ]
    return jnp.concatenate(pieces, axis=0)


def reorder(width):
    slots = width // BS
    source = lax.broadcasted_iota(jnp.int32, (width, width), 0)
    lane = lax.broadcasted_iota(jnp.int32, (width, width), 1)
    wanted = lane % BS // CHUNK * (slots * CHUNK) + lane // BS * CHUNK + lane % CHUNK
    return jnp.where(source == wanted, 1.0, 0.0).astype(bf16)


def select_chunk(read, chosen):
    rows = jnp.concatenate([read(o) for o in range(CHUNK)], axis=1)
    return dot(rows, chosen).astype(bf16)


def jac_blocks(slot, zg, yg, xg):
    c = slot // 2
    e = slot % 2
    d = c % 2
    kind = c // 2

    def block(z, y, x):
        return z * 16 + y * 4 + x

    own = block(2 * zg + kind % 2, 2 * yg + d, 2 * xg + e)
    below = block(jnp.maximum(2 * zg - 1, 0), 2 * yg + d, 2 * xg + e)
    above = block(jnp.minimum(2 * zg + 2, LAYERS - 1), 2 * yg + d, 2 * xg + e)
    beside = block(2 * zg + d, 2 - yg, 2 * xg + e)
    ahead = block(2 * zg + d, 2 * yg + e, 2 - xg)
    top = block(LAYERS - 1, 2 * yg + d, 2 * xg + e)
    bottom = block(0, 2 * yg + d, 2 * xg + e)
    result = own
    for at, choice in enumerate([below, above, beside, ahead, top, bottom]):
        result = jnp.where(kind == at + 2, choice, result)
    return result


def jac_kernel(jac, box, top, bottom):
    zg, yg, xg = box_of(lax.axis_index("tm"))
    width = 2 * COL
    perm = reorder(4 * width)
    tiles = []
    for tile in range(2):
        lane = lax.broadcasted_iota(jnp.int32, (1, width), 1)
        chosen = selector(jac_blocks(tile * 16 + lane // CHUNK, zg, yg, xg), width)
        chunks = [
            select_chunk(lambda o: jac[c * CHUNK + o], chosen) for c in range(BS // CHUNK)
        ]
        tiles.append(dot(jnp.concatenate(chunks, axis=1), perm).astype(bf16))
    box[:, : 8 * COL] = tiles[0]
    box[:, 8 * COL :] = tiles[1][:, : 4 * COL]
    top[...] = tiles[1][:, 4 * COL : 6 * COL]
    bottom[...] = tiles[1][:, 6 * COL :]


def select_jac(jac):
    edge = jax.ShapeDtypeStruct((BS, 2 * COL), bf16)
    return pl.pallas_call(
        jac_kernel,
        out_shape=(jax.ShapeDtypeStruct((BS, BOX), bf16), edge, edge),
        name="select_jac",
        cost_estimate=cost(10**9, 2 * 10**6),
    )(jac)


def ops_kernel(main, mass, out, chosen, picked):
    step = pl.program_id(0)
    zg, yg, xg = box_of(lax.axis_index("tm"))

    @pl.when(step == 0)
    def _():
        lane = lax.broadcasted_iota(jnp.int32, (1, COL), 1)
        slot = lane // CHUNK
        blocks = (
            (2 * zg + slot // 4) * 16 + (2 * yg + slot // 2 % 2) * 4 + 2 * xg + slot % 2
        )
        chosen[...] = selector(blocks, COL)

    for which, source in enumerate((main, mass)):
        picked[which, step] = select_chunk(lambda o: source[o], chosen[...])

    @pl.when(step == BS // CHUNK - 1)
    def _():
        perm = reorder(4 * COL)
        both = [
            dot(
                jnp.concatenate([picked[which, c] for c in range(BS // CHUNK)], axis=1), perm
            )
            for which in range(2)
        ]
        lane = lax.broadcasted_iota(jnp.int32, (BS, 2 * COL), 1)
        low = lane % COL < BS
        zero = jnp.zeros((BS, 2 * COL), f32)
        for dz in range(2):
            for dy in range(2):
                pair = 2 * dz + dy
                cut = slice(pair * COL, (pair + 1) * COL)
                slots = [
                    jnp.concatenate([b[s * BS : (s + 1) * BS, cut] for b in both], axis=1)
                    for s in range(SLOTS)
                ]

                def put(at, value):
                    out[pair, at * BS : (at + 1) * BS] = value.astype(bf16)

                def diagonal(at, value):
                    put(at, jnp.where(low, value, zero))
                    put(at + 1, jnp.where(low, zero, value))

                put(0, jnp.where(low, slots[0], slots[1]))
                put(1, jnp.where(low, slots[2], slots[0]))
                diagonal(2, slots[6 - dz])
                diagonal(4, slots[4 - dy])
                diagonal(6, slots[5 + dz])
                faces = (yg == 1) if dy == 0 else (yg == 0)
                diagonal(8, slots[3 + dy] * jnp.where(faces, 1.0, 0.0))
                after = jnp.where(xg == 0, 1.0, 0.0)
                put(
                    10 + dy,
                    jnp.where(low, slots[1] * (1.0 - after), slots[2] * after),
                )
                put(11 - dy, zero)


def select_ops(main, mass):
    spec = pl.BlockSpec((CHUNK, SLOTS * BS, BLOCKS), lambda c: (c, 0, 0))
    return pl.pallas_call(
        ops_kernel,
        grid=(BS // CHUNK,),
        in_specs=[spec, spec],
        out_specs=pl.BlockSpec((4, 6 * COL, 2 * COL), lambda c: (0, 0, 0)),
        out_shape=jax.ShapeDtypeStruct((4, 6 * COL, 2 * COL), bf16),
        scratch_shapes=[
            pltpu.VMEM((CHUNK * BLOCKS, COL), bf16),
            pltpu.VMEM((2, BS // CHUNK, SLOTS * BS, COL), bf16),
        ],
        name="select_ops",
        compiler_params=pltpu.CompilerParams(vmem_limit_bytes=40 * 2**20),
        cost_estimate=cost(4 * 10**9, 16 * 10**6),
    )(main, mass)


def solve_kernel(recv, ops, box, from_low, from_high, table, out):
    zg, _, _ = box_of(lax.axis_index("tm"))
    low = lax.broadcasted_iota(jnp.int32, (BS, COL), 1) < BS
    zero = jnp.zeros((BS, COL), bf16)

    def fields(c):
        return recv[:, c * COL : (c + 1) * COL]

    def inverse(c):
        value = box[:, c * COL : (c + 1) * COL]
        if c in (4, 5):
            value = jnp.where(zg == 0, from_low[:, (c - 4) * COL : (c - 3) * COL], value)
        if c in (6, 7):
            value = jnp.where(zg == 3, from_high[:, (c - 6) * COL : (c - 5) * COL], value)
        return jnp.concatenate(
            [jnp.where(low, value, zero), jnp.where(low, zero, value)], axis=0
        )

    inverses = [inverse(c) for c in range(4)]
    firsts = [dot(fields(c), inverses[c]) for c in range(4)]
    lows = [value.astype(bf16) for value in firsts]
    lows += [dot(fields(c), inverse(c)).astype(bf16) for c in range(4, 12)]

    ids = step_ids(0, LENGTH, COL).astype(f32)
    growth = jnp.exp(ids * -LOG_STEP)
    seconds = []
    for dz in range(2):
        for dy in range(2):
            pair = 2 * dz + dy
            around = jnp.concatenate(
                [
                    lows[pair],
                    lows[2 - 2 * dz + dy],
                    lows[2 * dz + 1 - dy],
                    lows[4 + 2 * dz + dy],
                    lows[8 + dz],
                    lows[10 + dz],
                ],
                axis=1,
            )
            image = dot(around, ops[pair])
            earlier = pltpu.roll(image[:, COL:], 1, 0)
            residue = fields(pair).astype(f32) - image[:, :COL] + MODULUS * earlier
            second = firsts[pair] + dot(residue.astype(bf16), inverses[pair])
            in_time = (second * growth).astype(bf16)
            for dest in range(PARTS):
                out[dest, 2 * STEPS :, pair * COL : (pair + 1) * COL] = in_time[
                    dest * STEPS : (dest + 1) * STEPS
                ]
            seconds.append(second)
    second = jnp.concatenate(seconds, axis=1)
    high = second.astype(bf16)
    rest = (second - high.astype(f32)).astype(bf16)
    spectrum = dot(table[...], jnp.concatenate([high, rest, high], axis=0)).astype(bf16)
    for dest in range(PARTS):
        out[dest, : 2 * STEPS] = spectrum[dest * 2 * STEPS : (dest + 1) * 2 * STEPS]


def solve(recv, ops, box, from_low, from_high):
    return pl.pallas_call(
        solve_kernel,
        out_shape=jax.ShapeDtypeStruct((PARTS, 3 * STEPS, OWN), bf16),
        name="solve",
        compiler_params=pltpu.CompilerParams(vmem_limit_bytes=40 * 2**20),
        cost_estimate=cost(3 * 10**9, 5 * 10**6),
    )(recv, ops, box, from_low, from_high, jnp.asarray(dft_table()))


def unpack_kernel(recv, real, imag, in_time):
    for source in range(PARTS):
        zg, yg, xg = box_of(source)
        for d in range(2):
            for e in range(2):
                at = (2 * zg + d) * LAYER + (2 * yg + e) * ROW + xg * COL
                c = 2 * d + e
                for which, out in enumerate((real, imag, in_time)):
                    out[:, at : at + COL] = recv[
                        source,
                        which * STEPS : (which + 1) * STEPS,
                        c * COL : (c + 1) * COL,
                    ].astype(f32)


def unpack(recv):
    out = jax.ShapeDtypeStruct((STEPS, SLAB), f32)
    return pl.pallas_call(
        unpack_kernel,
        out_shape=(out, out, out),
        name="unpack",
        cost_estimate=cost(10**6, 3 * 10**6),
    )(recv)


def per_device(forcing, op_main, op_mass, jacobi_inv):
    count = lax.axis_size("space")
    up = [(i, i + 1) for i in range(count - 1)]
    down = [(i + 1, i) for i in range(count - 1)]
    local_ids = lax.axis_index("tm") * STEPS + jnp.arange(STEPS, dtype=jnp.int32)
    scale = jnp.exp(local_ids.astype(f32) * LOG_STEP)[:, None]
    bottom = (forcing[:, :LAYER] * scale).astype(bf16)
    top = (forcing[:, SLAB - LAYER :] * scale).astype(bf16)
    low_edge = lax.ppermute(top, "space", up)
    high_edge = lax.ppermute(bottom, "space", down)

    box, jac_top, jac_bottom = select_jac(jnp.transpose(jacobi_inv, (1, 2, 0)))
    packed = pack(forcing, low_edge, high_edge)
    packed, jac_top, jac_bottom = lax.optimization_barrier((packed, jac_top, jac_bottom))
    recv = lax.all_to_all(packed, "tm", 0, 0).reshape(LENGTH, BOX)
    from_low = lax.ppermute(jac_top, "space", up)
    from_high = lax.ppermute(jac_bottom, "space", down)
    ops = select_ops(jnp.transpose(op_main, (1, 2, 0)), jnp.transpose(op_mass, (1, 2, 0)))
    sent = solve(recv, ops, box, from_low, from_high)
    back = lax.all_to_all(sent, "tm", 0, 0)
    return unpack(back)


def solution(mesh):
    in_specs = (
        P("tm", "space"),
        P("space", None, None),
        P("space", None, None),
        P("space", None, None),
    )
    out_specs = (P("tm", "space"), P("tm", "space"), P("tm", "space"))
    return jax.shard_map(
        per_device, mesh=mesh, in_specs=in_specs, out_specs=out_specs, check_vma=False
    )
```

profile of v0, /device:TPU:32, one launch (start us, length us, event | category | flops | bytes accessed | tf_op | source)
XLA Modules:
  0.0 63.2 jit_solution(10249615264302741236)
XLA Ops:
  0.6 1.0 %multiply_convert_fusion = (bf16[16,1024]{1,0:T(8,128)(2,1)S(1)}, bf16[16,1024]{1,0:T(8,128)(2,1)S(1)}) fusion(f32[16,8192]{1,0:T(8,128)} %forcing.1, f32[16]{0:T(128)S(1)} %multiply_exponential_fusion), kind=kLoop, calls=%fused_computation | loop fusion | flops 65536 | bytes 196672 | tf_op jit(solution)/shard_map/convert_element_type | solution.py:364
  1.6 1.9 %collective-permute-start.1 = (bf16[16,1024]{1,0:T(8,128)(2,1)S(1)}, bf16[16,1024]{1,0:T(8,128)(2,1)S(1)}, u32[]{:S(2)}, u32[]{:S(2)}) collective-permute-start(bf16[16,1024]{1,0:T(8,128)(2,1)S(1)} %get-tuple-element.15), channel_id=1, source_target_pairs={{1,0},{2,1},{3,2},{4,3},{5,4},{6,5},{7,6},{9,8},{10,9},{11,10},{12... | collective-permute-start | bytes 98312 | tf_op jit(solution)/shard_map/ppermute | solution.py:367
  3.5 2.4 %collective-permute-start = (bf16[16,1024]{1,0:T(8,128)(2,1)S(1)}, bf16[16,1024]{1,0:T(8,128)(2,1)S(1)}, u32[]{:S(2)}, u32[]{:S(2)}) collective-permute-start(bf16[16,1024]{1,0:T(8,128)(2,1)S(1)} %get-tuple-element.16), channel_id=1, source_target_pairs={{0,1},{1,2},{2,3},{3,4},{4,5},{5,6},{6,7},{8,9},{9,10},{10,11},{11... | collective-permute-start | bytes 98312 | tf_op jit(solution)/shard_map/ppermute | solution.py:366
  5.9 4.5 %select_jac.1 = (bf16[64,1536]{1,0:T(8,128)(2,1)}, bf16[64,256]{1,0:T(8,128)(2,1)}, bf16[64,256]{1,0:T(8,128)(2,1)}) custom-call(bf16[64,64,128]{2,1,0:T(8,128)(2,1)} %bitcast.7), custom_call_target="tpu_custom_call" | custom-call | flops 1000000000 | bytes 2000000 | tf_op jit(solution)/shard_map/select_jac/pallas_call | solution.py:180
  10.5 0.0 collective-permute-done.1.high_edge
  10.5 0.0 copy-start.3
  10.5 0.0 collective-permute-done.low_edge
  10.5 0.6 copy-done.3
  11.1 0.6 copy-done.4
  11.7 2.1 %pack.1 = bf16[16,16,1536]{2,1,0:T(8,128)(2,1)} custom-call(f32[16,8192]{1,0:T(8,128)} %forcing.1, bf16[16,1024]{1,0:T(8,128)(2,1)} %copy-done.4, bf16[16,1024]{1,0:T(8,128)(2,1)} %copy-done.3), custom_call_target="tpu_custom_call" | custom-call | flops 1000000 | bytes 2000000 | tf_op jit(solution)/shard_map/pack/pallas_call | solution.py:107
  13.8 7.0 %all-to-all-start = ((bf16[16,16,1536]{2,1,0:T(8,128)(2,1)}), bf16[16,16,1536]{2,1,0:T(8,128)(2,1)S(1)}, u32[]{:S(2)}, u32[]{:S(2)}) async-start(bf16[16,16,1536]{2,1,0:T(8,128)(2,1)} %pack.1), calls=%async_computation | async-start | bytes 1572864 | tf_op jit(solution)/shard_map/all_to_all | solution.py:372
  20.8 3.2 %collective-permute-start.2 = (bf16[64,256]{1,0:T(8,128)(2,1)}, bf16[64,256]{1,0:T(8,128)(2,1)S(1)}, u32[]{:S(2)}, u32[]{:S(2)}) collective-permute-start(bf16[64,256]{1,0:T(8,128)(2,1)} %get-tuple-element.13), channel_id=1, source_target_pairs={{0,1},{1,2},{2,3},{3,4},{4,5},{5,6},{6,7},{8,9},{9,10},{10,11},{11... | collective-permute-start | bytes 98312 | tf_op jit(solution)/shard_map/ppermute | solution.py:373
  24.0 2.4 %collective-permute-start.3 = (bf16[64,256]{1,0:T(8,128)(2,1)}, bf16[64,256]{1,0:T(8,128)(2,1)S(1)}, u32[]{:S(2)}, u32[]{:S(2)}) collective-permute-start(bf16[64,256]{1,0:T(8,128)(2,1)} %get-tuple-element.14), channel_id=1, source_target_pairs={{1,0},{2,1},{3,2},{4,3},{5,4},{6,5},{7,6},{9,8},{10,9},{11,10},{12... | collective-permute-start | bytes 98312 | tf_op jit(solution)/shard_map/ppermute | solution.py:374
  26.4 0.0 copy-start
  26.4 3.1 %copy-done = bf16[128,64,448]{0,2,1:T(8,128)(2,1)S(1)} copy-done((bf16[128,64,448]{0,2,1:T(8,128)(2,1)S(1)}, bf16[128,64,448]{0,2,1:T(8,128)(2,1)}, u32[]{:S(2)}) %copy-start) | copy-done | bytes 7340056
  29.5 7.4 %select_ops.1.ops = bf16[4,768,256]{2,1,0:T(8,128)(2,1)S(1)} custom-call(bf16[64,448,128]{2,1,0:T(8,128)(2,1)S(1)} %bitcast.4, bf16[64,448,128]{2,1,0:T(8,128)(2,1)} %bitcast.6), custom_call_target="tpu_custom_call" | custom-call | flops 4000000000 | bytes 16000000 | tf_op jit(solution)/shard_map/select_ops/pallas_call | solution.py:249
  36.9 0.0 collective-permute-done.2.from_low
  36.9 0.0 collective-permute-done.3.from_high
  36.9 0.0 all-to-all-done
  36.9 0.0 copy-done.1
  36.9 0.0 copy-done.2
  36.9 2.3 %solve.1 = bf16[16,48,512]{2,1,0:T(8,128)(2,1)S(1)} custom-call(bf16[256,1536]{1,0:T(8,128)(2,1)S(1)} %bitcast.5, bf16[4,768,256]{2,1,0:T(8,128)(2,1)S(1)} %select_ops.1.ops, bf16[64,1536]{1,0:T(8,128)(2,1)S(1)} %copy-done.2, bf16[64,256]{1,0:T(8,128)(2,1)S(1)} %collective-permute-done.2.from_low, bf16[64,256]{1,0:T(8,128)(2,1)S(1)} %collective-permute-done.3.from_high, ...), custom_call_target="tpu_custom_call" | custom-call | flops 3000000000 | bytes 5000000 | tf_op jit(solution)/shard_map/solve/pallas_call | solution.py:324
  39.2 21.7 %all_to_all.10.recv = bf16[16,48,512]{2,1,0:T(8,128)(2,1)} all-to-all(bf16[16,48,512]{2,1,0:T(8,128)(2,1)S(1)} %solve.1), channel_id=1, replica_groups=mesh['tm'=16,'space'=8] {'tm'}, dimensions={0} | all-to-all | bytes 1572864 | tf_op jit(solution)/shard_map/all_to_all | solution.py:377
  60.9 2.3 %unpack.1 = (f32[16,8192]{1,0:T(8,128)}, f32[16,8192]{1,0:T(8,128)}, f32[16,8192]{1,0:T(8,128)}) custom-call(bf16[16,48,512]{2,1,0:T(8,128)(2,1)} %all_to_all.10.recv), custom_call_target="tpu_custom_call" | custom-call | flops 1000000 | bytes 3000000 | tf_op jit(solution)/shard_map/unpack/pallas_call | solution.py:350
  (4 shorter events, 0.0 us)
Async XLA Ops:
  1.6 8.9 %collective-permute-start.1 = (bf16[16,1024]{1,0:T(8,128)(2,1)S(1)}, bf16[16,1024]{1,0:T(8,128)(2,1)S(1)}, u32[]{:S(2)}, u32[]{:S(2)}) collective-permute-start(bf16[16,1024]{1,0:T(8,128)(2,1)S(1)} %get-tuple-element.15), channel_id=1, source_target_pairs={{1,0},{2,1},{3,2},{4,3},{5,4},{6,5},{7,6},{9,8},{10,9},{11,10},{12... | collective-permute-start | bytes 98312 | tf_op jit(solution)/shard_map/ppermute | solution.py:367
  3.5 6.9 %collective-permute-start = (bf16[16,1024]{1,0:T(8,128)(2,1)S(1)}, bf16[16,1024]{1,0:T(8,128)(2,1)S(1)}, u32[]{:S(2)}, u32[]{:S(2)}) collective-permute-start(bf16[16,1024]{1,0:T(8,128)(2,1)S(1)} %get-tuple-element.16), channel_id=1, source_target_pairs={{0,1},{1,2},{2,3},{3,4},{4,5},{5,6},{6,7},{8,9},{9,10},{10,11},{11... | collective-permute-start | bytes 98312 | tf_op jit(solution)/shard_map/ppermute | solution.py:366
  10.5 0.6 copy-start.3
  11.1 0.6 copy-start.4
  13.8 23.1 %all-to-all-start = ((bf16[16,16,1536]{2,1,0:T(8,128)(2,1)}), bf16[16,16,1536]{2,1,0:T(8,128)(2,1)S(1)}, u32[]{:S(2)}, u32[]{:S(2)}) async-start(bf16[16,16,1536]{2,1,0:T(8,128)(2,1)} %pack.1), calls=%async_computation | async-start | bytes 1572864 | tf_op jit(solution)/shard_map/all_to_all | solution.py:372
  20.8 16.1 %collective-permute-start.2 = (bf16[64,256]{1,0:T(8,128)(2,1)}, bf16[64,256]{1,0:T(8,128)(2,1)S(1)}, u32[]{:S(2)}, u32[]{:S(2)}) collective-permute-start(bf16[64,256]{1,0:T(8,128)(2,1)} %get-tuple-element.13), channel_id=1, source_target_pairs={{0,1},{1,2},{2,3},{3,4},{4,5},{5,6},{6,7},{8,9},{9,10},{10,11},{11... | collective-permute-start | bytes 98312 | tf_op jit(solution)/shard_map/ppermute | solution.py:373
  24.0 12.9 %collective-permute-start.3 = (bf16[64,256]{1,0:T(8,128)(2,1)}, bf16[64,256]{1,0:T(8,128)(2,1)S(1)}, u32[]{:S(2)}, u32[]{:S(2)}) collective-permute-start(bf16[64,256]{1,0:T(8,128)(2,1)} %get-tuple-element.14), channel_id=1, source_target_pairs={{1,0},{2,1},{3,2},{4,3},{5,4},{6,5},{7,6},{9,8},{10,9},{11,10},{12... | collective-permute-start | bytes 98312 | tf_op jit(solution)/shard_map/ppermute | solution.py:374
  26.4 3.1 %copy-start = (bf16[128,64,448]{0,2,1:T(8,128)(2,1)S(1)}, bf16[128,64,448]{0,2,1:T(8,128)(2,1)}, u32[]{:S(2)}) copy-start(bf16[128,64,448]{0,2,1:T(8,128)(2,1)} %param.6) | copy-start | bytes 22020100
  29.5 7.4 %copy-start.1 = (bf16[512,768]{1,0:T(8,128)(2,1)S(1)}, bf16[512,768]{1,0:T(8,128)(2,1)}, u32[]{:S(2)}) copy-start(bf16[512,768]{1,0:T(8,128)(2,1)} %constant.12.clone.table) | copy-start | bytes 2359300
  29.5 7.4 %copy-start.2 = (bf16[64,1536]{1,0:T(8,128)(2,1)S(1)}, bf16[64,1536]{1,0:T(8,128)(2,1)}, u32[]{:S(2)}) copy-start(bf16[64,1536]{1,0:T(8,128)(2,1)} %get-tuple-element.12.box) | copy-start | bytes 589828
where the time goes:
time: 64 us; the launch traced here: 63.2 us
  blocking collectives  21.7 us (34%)
  Pallas kernels  18.6 us (29%)
  starting transfers between devices  16.9 us (26%)
  local copies, waits for them, and re-layouts  4.31 us (7%)
  other arithmetic  0.96 us (2%)
  between operations  0.75 us (1%)
    all_to_all x1, blocking collectives, per_device(): back = lax.all_to_all(sent, 'tm', 0, 0)  21.7 us
    pallas_call x1, Pallas kernels, select_ops(): pl.pallas_call(ops_kernel, grid=(BS // CHUNK,), in_specs=[spec, spec], ou...  7.38 us
    all_to_all x1, starting transfers between devices, per_device(): recv = lax.all_to_all(packed, 'tm', 0, 0).reshape(LENGTH, BOX)  7.03 us
    pallas_call x1, Pallas kernels, select_jac(): pl.pallas_call(jac_kernel, out_shape=(jax.ShapeDtypeStruct((BS, BOX), bf1...  4.52 us
    unnamed x10, local copies, waits for them, and re-layouts  4.31 us
    ppermute x1, starting transfers between devices, per_device(): from_low = lax.ppermute(jac_top, 'space', up)  3.16 us
    ppermute x1, starting transfers between devices, per_device(): low_edge = lax.ppermute(top, 'space', up)  2.41 us
    ppermute x1, starting transfers between devices, per_device(): from_high = lax.ppermute(jac_bottom, 'space', down)  2.4 us
  transfers between devices with their start and end apart: 5, of which 0 were waited for; matrix products, arithmetic and copies ran while one was open for 0% of the time, Pallas kernels for 19%

commit v1 on v0

--- a/solution.py
+++ b/solution.py
@@ -61,18 +61,28 @@
     return jnp.dot(a, b, preferred_element_type=f32)
 
 
-def pack_kernel(forcing, low_edge, high_edge, out):
-    part = lax.axis_index("tm")
-    ids = step_ids(part, STEPS, COL).astype(f32)
-    scale = jnp.exp(ids * LOG_STEP)
+def scales():
+    ids = step_ids(lax.axis_index("tm"), STEPS, COL).astype(f32)
+    return jnp.exp(ids * LOG_STEP)
+
+
+def pack_kernel(source, out, forcing, sems):
+    copies = []
+    for group in range(4):
+        cut = pl.ds(group * 2 * LAYER, 2 * LAYER)
+        copies.append(
+            pltpu.make_async_copy(source.at[:, cut], forcing.at[:, cut], sems.at[group])
+        )
+    for copy in copies:
+        copy.start()
+    for copy in copies:
+        copy.wait()
+    scale = scales()
     half = lax.broadcasted_iota(jnp.int32, (STEPS, COL), 1) < BS
-    cols = {}
 
     def column(z, y, x):
         at = z * LAYER + y * ROW + x * COL
-        if at not in cols:
-            cols[at] = forcing[:, at : at + COL] * scale
-        return cols[at]
+        return forcing[:, at : at + COL] * scale
 
     def put(dest, c, value):
         out[dest, :, c * COL : (c + 1) * COL] = value.astype(bf16)
@@ -83,14 +93,9 @@
             for e in range(2):
                 put(dest, 2 * d + e, column(2 * zg + d, 2 * yg + e, xg))
             y = 2 * yg + d
-            at = y * ROW + xg * COL
-            if zg == 0:
-                put(dest, 4 + d, low_edge[:, at : at + COL])
-            else:
+            if zg > 0:
                 put(dest, 4 + d, column(2 * zg - 1, y, xg))
-            if zg == 3:
-                put(dest, 6 + d, high_edge[:, at : at + COL])
-            else:
+            if zg < 3:
                 put(dest, 6 + d, column(2 * zg + 2, y, xg))
             z = 2 * zg + d
             put(dest, 8 + d, column(z, 2 - yg, xg))
@@ -103,13 +108,52 @@
             put(dest, 10 + d, pair)
 
 
-def pack(forcing, low_edge, high_edge):
+def pack(forcing):
     return pl.pallas_call(
         pack_kernel,
+        in_specs=[pl.BlockSpec(memory_space=pltpu.HBM)],
         out_shape=jax.ShapeDtypeStruct((PARTS, STEPS, BOX), bf16),
+        scratch_shapes=[pltpu.VMEM((STEPS, SLAB), f32), pltpu.SemaphoreType.DMA((4,))],
         name="pack",
-        cost_estimate=cost(10**6, 2 * 10**6),
-    )(forcing, low_edge, high_edge)
+        compiler_params=pltpu.CompilerParams(vmem_limit_bytes=6 * 2**20),
+        cost_estimate=cost(10**6, 4 * 10**6),
+    )(forcing)
+
+
+def patch_kernel(packed, low_edge, high_edge, out, sems):
+    copies = []
+    for dest in range(PARTS):
+        zg, yg, xg = box_of(dest)
+        for edge, at_group, first in ((low_edge, 0, 4), (high_edge, 3, 6)):
+            if zg == at_group:
+                for d in range(2):
+                    at = (2 * yg + d) * ROW + xg * COL
+                    copies.append(
+                        pltpu.make_async_copy(
+                            edge.at[pl.ds(0, STEPS), pl.ds(at, COL)],
+                            out.at[dest, :, pl.ds((first + d) * COL, COL)],
+                            sems.at[len(copies)],
+                        )
+                    )
+    for copy in copies:
+        copy.start()
+    for copy in copies:
+        copy.wait()
+
+
+def patch(packed, low_edge, high_edge):
+    anywhere = pl.BlockSpec(memory_space=pl.ANY)
+    return pl.pallas_call(
+        patch_kernel,
+        in_specs=[anywhere] * 3,
+        out_specs=anywhere,
+        out_shape=jax.ShapeDtypeStruct((PARTS, STEPS, BOX), bf16),
+        scratch_shapes=[pltpu.SemaphoreType.DMA((16,))],
+        input_output_aliases={0: 0},
+        name="patch",
+        compiler_params=pltpu.CompilerParams(vmem_limit_bytes=2**20),
+        cost_estimate=cost(10**3, 2 * 10**5),
+    )(packed, low_edge, high_edge)
 
 
 def selector(blocks, width):
@@ -135,52 +179,102 @@
     return dot(rows, chosen).astype(bf16)
 
 
-def jac_blocks(slot, zg, yg, xg):
-    c = slot // 2
+def select_all(jac, blocks, perm):
+    chunks = BS // CHUNK
+    rows = jnp.concatenate(
+        [
+            jnp.concatenate([jac[c * CHUNK + o] for c in range(chunks)], axis=0)
+            for o in range(CHUNK)
+        ],
+        axis=1,
+    )
+    picked = dot(rows, selector(blocks, COL)).astype(bf16)
+    side = jnp.concatenate([picked[c * BS : (c + 1) * BS] for c in range(chunks)], axis=1)
+    return dot(side, perm).astype(bf16)
+
+
+def slots_of():
+    return lax.broadcasted_iota(jnp.int32, (1, COL), 1) // CHUNK
+
+
+def block_at(z, y, x):
+    return z * 16 + y * 4 + x
+
+
+def edge_kernel(forcing, jac, top, bottom, ends, local, sems):
+    copies = [
+        pltpu.make_async_copy(jac, local, sems.at[0]),
+        pltpu.make_async_copy(forcing.at[:, pl.ds(0, LAYER)], ends.at[0], sems.at[1]),
+        pltpu.make_async_copy(
+            forcing.at[:, pl.ds(SLAB - LAYER, LAYER)], ends.at[1], sems.at[2]
+        ),
+    ]
+    for copy in copies:
+        copy.start()
+    _, yg, xg = box_of(lax.axis_index("tm"))
+    scale = jnp.concatenate([scales()] * (LAYER // COL), axis=1)
+    slot = slots_of()
+    layer = jnp.where(slot < 4, LAYERS - 1, 0)
+    blocks = block_at(layer, 2 * yg + slot // 2 % 2, 2 * xg + slot % 2)
+    perm = reorder(4 * COL)
+    for copy in copies:
+        copy.wait()
+    bottom[:STEPS] = (ends[0] * scale).astype(bf16)
+    top[:STEPS] = (ends[1] * scale).astype(bf16)
+    picked = select_all(local, blocks, perm)
+    for a in range(BS // STEPS):
+        cut = slice(a * 2 * COL, (a + 1) * 2 * COL)
+        top[STEPS:, cut] = picked[a * STEPS : (a + 1) * STEPS, : 2 * COL]
+        bottom[STEPS:, cut] = picked[a * STEPS : (a + 1) * STEPS, 2 * COL :]
+
+
+def edges(forcing, jac):
+    edge = jax.ShapeDtypeStruct((2 * STEPS, LAYER), bf16)
+    hbm = pl.BlockSpec(memory_space=pltpu.HBM)
+    return pl.pallas_call(
+        edge_kernel,
+        in_specs=[hbm, hbm],
+        out_shape=(edge, edge),
+        scratch_shapes=[
+            pltpu.VMEM((2, STEPS, LAYER), f32),
+            pltpu.VMEM((BS, BS, BLOCKS), bf16),
+            pltpu.SemaphoreType.DMA((3,)),
+        ],
+        name="edges",
+        compiler_params=pltpu.CompilerParams(vmem_limit_bytes=63 * 10**6),
+        cost_estimate=cost(10**8, 2 * 10**6),
+    )(forcing, jac)
+
+
+def jac_kernel(jac, box, local, sem):
+    copy = pltpu.make_async_copy(jac, local, sem)
+    copy.start()
+    zg, yg, xg = box_of(lax.axis_index("tm"))
+    slot = slots_of()
+    d = slot // 2 % 2
     e = slot % 2
-    d = c % 2
-    kind = c // 2
-
-    def block(z, y, x):
-        return z * 16 + y * 4 + x
-
-    own = block(2 * zg + kind % 2, 2 * yg + d, 2 * xg + e)
-    below = block(jnp.maximum(2 * zg - 1, 0), 2 * yg + d, 2 * xg + e)
-    above = block(jnp.minimum(2 * zg + 2, LAYERS - 1), 2 * yg + d, 2 * xg + e)
-    beside = block(2 * zg + d, 2 - yg, 2 * xg + e)
-    ahead = block(2 * zg + d, 2 * yg + e, 2 - xg)
-    top = block(LAYERS - 1, 2 * yg + d, 2 * xg + e)
-    bottom = block(0, 2 * yg + d, 2 * xg + e)
-    result = own
-    for at, choice in enumerate([below, above, beside, ahead, top, bottom]):
-        result = jnp.where(kind == at + 2, choice, result)
-    return result
-
-
-def jac_kernel(jac, box, top, bottom):
-    zg, yg, xg = box_of(lax.axis_index("tm"))
-    width = 2 * COL
-    perm = reorder(4 * width)
-    tiles = []
-    for tile in range(2):
-        lane = lax.broadcasted_iota(jnp.int32, (1, width), 1)
-        chosen = selector(jac_blocks(tile * 16 + lane // CHUNK, zg, yg, xg), width)
-        chunks = [
-            select_chunk(lambda o: jac[c * CHUNK + o], chosen) for c in range(BS // CHUNK)
-        ]
-        tiles.append(dot(jnp.concatenate(chunks, axis=1), perm).astype(bf16))
-    box[:, : 8 * COL] = tiles[0]
-    box[:, 8 * COL :] = tiles[1][:, : 4 * COL]
-    top[...] = tiles[1][:, 4 * COL : 6 * COL]
-    bottom[...] = tiles[1][:, 6 * COL :]
+    first = slot < 4
+    own = block_at(2 * zg + slot // 4, 2 * yg + d, 2 * xg + e)
+    layer = jnp.where(
+        first, jnp.maximum(2 * zg - 1, 0), jnp.minimum(2 * zg + 2, LAYERS - 1)
+    )
+    faces = block_at(layer, 2 * yg + d, 2 * xg + e)
+    beside = block_at(2 * zg + d, 2 - yg, 2 * xg + e)
+    ahead = block_at(2 * zg + d, 2 * yg + e, 2 - xg)
+    perm = reorder(4 * COL)
+    copy.wait()
+    for at, blocks in enumerate((own, faces, jnp.where(first, beside, ahead))):
+        box[:, at * 4 * COL : (at + 1) * 4 * COL] = select_all(local, blocks, perm)
 
 
 def select_jac(jac):
-    edge = jax.ShapeDtypeStruct((BS, 2 * COL), bf16)
     return pl.pallas_call(
         jac_kernel,
-        out_shape=(jax.ShapeDtypeStruct((BS, BOX), bf16), edge, edge),
+        in_specs=[pl.BlockSpec(memory_space=pltpu.HBM)],
+        out_shape=jax.ShapeDtypeStruct((BS, BOX), bf16),
+        scratch_shapes=[pltpu.VMEM((BS, BS, BLOCKS), bf16), pltpu.SemaphoreType.DMA],
         name="select_jac",
+        compiler_params=pltpu.CompilerParams(vmem_limit_bytes=63 * 10**6),
         cost_estimate=cost(10**9, 2 * 10**6),
     )(jac)
 
@@ -191,11 +285,8 @@
 
     @pl.when(step == 0)
     def _():
-        lane = lax.broadcasted_iota(jnp.int32, (1, COL), 1)
-        slot = lane // CHUNK
-        blocks = (
-            (2 * zg + slot // 4) * 16 + (2 * yg + slot // 2 % 2) * 4 + 2 * xg + slot % 2
-        )
+        slot = slots_of()
+        blocks = block_at(2 * zg + slot // 4, 2 * yg + slot // 2 % 2, 2 * xg + slot % 2)
         chosen[...] = selector(blocks, COL)
 
     for which, source in enumerate((main, mass)):
@@ -257,12 +348,12 @@
             pltpu.VMEM((2, BS // CHUNK, SLOTS * BS, COL), bf16),
         ],
         name="select_ops",
-        compiler_params=pltpu.CompilerParams(vmem_limit_bytes=40 * 2**20),
+        compiler_params=pltpu.CompilerParams(vmem_limit_bytes=52 * 2**20),
         cost_estimate=cost(4 * 10**9, 16 * 10**6),
     )(main, mass)
 
 
-def solve_kernel(recv, ops, box, from_low, from_high, table, out):
+def solve_kernel(recv, ops, box, low_edge, high_edge, table, out):
     zg, _, _ = box_of(lax.axis_index("tm"))
     low = lax.broadcasted_iota(jnp.int32, (BS, COL), 1) < BS
     zero = jnp.zeros((BS, COL), bf16)
@@ -270,12 +361,18 @@
     def fields(c):
         return recv[:, c * COL : (c + 1) * COL]
 
+    def other(edge, d):
+        pieces = [
+            edge[STEPS:, (2 * a + d) * COL : (2 * a + d + 1) * COL] for a in range(BS // STEPS)
+        ]
+        return jnp.concatenate(pieces, axis=0)
+
     def inverse(c):
         value = box[:, c * COL : (c + 1) * COL]
         if c in (4, 5):
-            value = jnp.where(zg == 0, from_low[:, (c - 4) * COL : (c - 3) * COL], value)
+            value = jnp.where(zg == 0, other(low_edge, c - 4), value)
         if c in (6, 7):
-            value = jnp.where(zg == 3, from_high[:, (c - 6) * COL : (c - 5) * COL], value)
+            value = jnp.where(zg == 3, other(high_edge, c - 6), value)
         return jnp.concatenate(
             [jnp.where(low, value, zero), jnp.where(low, zero, value)], axis=0
         )
@@ -320,29 +417,40 @@
         out[dest, : 2 * STEPS] = spectrum[dest * 2 * STEPS : (dest + 1) * 2 * STEPS]
 
 
-def solve(recv, ops, box, from_low, from_high):
+def solve(recv, ops, box, low_edge, high_edge):
     return pl.pallas_call(
         solve_kernel,
         out_shape=jax.ShapeDtypeStruct((PARTS, 3 * STEPS, OWN), bf16),
         name="solve",
         compiler_params=pltpu.CompilerParams(vmem_limit_bytes=40 * 2**20),
         cost_estimate=cost(3 * 10**9, 5 * 10**6),
-    )(recv, ops, box, from_low, from_high, jnp.asarray(dft_table()))
-
-
-def unpack_kernel(recv, real, imag, in_time):
-    for source in range(PARTS):
-        zg, yg, xg = box_of(source)
-        for d in range(2):
-            for e in range(2):
-                at = (2 * zg + d) * LAYER + (2 * yg + e) * ROW + xg * COL
-                c = 2 * d + e
-                for which, out in enumerate((real, imag, in_time)):
-                    out[:, at : at + COL] = recv[
-                        source,
-                        which * STEPS : (which + 1) * STEPS,
-                        c * COL : (c + 1) * COL,
-                    ].astype(f32)
+    )(recv, ops, box, low_edge, high_edge, jnp.asarray(dft_table()))
+
+
+def unpack_kernel(recv, real, imag, in_time, ready, sems):
+    copies = []
+    for zg in range(4):
+        for which, out in enumerate((real, imag, in_time)):
+            for d in range(2):
+                for rest in range(4):
+                    source = 4 * zg + rest
+                    _, yg, xg = box_of(source)
+                    for e in range(2):
+                        at = (2 * zg + d) * LAYER + (2 * yg + e) * ROW + xg * COL
+                        c = 2 * d + e
+                        ready[which, :, at : at + COL] = recv[
+                            source,
+                            which * STEPS : (which + 1) * STEPS,
+                            c * COL : (c + 1) * COL,
+                        ].astype(f32)
+            cut = pl.ds(2 * zg * LAYER, 2 * LAYER)
+            copy = pltpu.make_async_copy(
+                ready.at[which, :, cut], out.at[:, cut], sems.at[len(copies)]
+            )
+            copy.start()
+            copies.append(copy)
+    for copy in copies:
+        copy.wait()
 
 
 def unpack(recv):
@@ -350,7 +458,10 @@
     return pl.pallas_call(
         unpack_kernel,
         out_shape=(out, out, out),
+        out_specs=(pl.BlockSpec(memory_space=pltpu.HBM),) * 3,
+        scratch_shapes=[pltpu.VMEM((3, STEPS, SLAB), f32), pltpu.SemaphoreType.DMA((12,))],
         name="unpack",
+        compiler_params=pltpu.CompilerParams(vmem_limit_bytes=6 * 2**20),
         cost_estimate=cost(10**6, 3 * 10**6),
     )(recv)
 
@@ -359,21 +470,18 @@
     count = lax.axis_size("space")
     up = [(i, i + 1) for i in range(count - 1)]
     down = [(i + 1, i) for i in range(count - 1)]
-    local_ids = lax.axis_index("tm") * STEPS + jnp.arange(STEPS, dtype=jnp.int32)
-    scale = jnp.exp(local_ids.astype(f32) * LOG_STEP)[:, None]
-    bottom = (forcing[:, :LAYER] * scale).astype(bf16)
-    top = (forcing[:, SLAB - LAYER :] * scale).astype(bf16)
+    jac = jnp.transpose(jacobi_inv, (1, 2, 0))
+    top, bottom = edges(forcing, jac)
     low_edge = lax.ppermute(top, "space", up)
     high_edge = lax.ppermute(bottom, "space", down)
-
-    box, jac_top, jac_bottom = select_jac(jnp.transpose(jacobi_inv, (1, 2, 0)))
-    packed = pack(forcing, low_edge, high_edge)
-    packed, jac_top, jac_bottom = lax.optimization_barrier((packed, jac_top, jac_bottom))
+    packed = pack(forcing)
+    low_edge, high_edge, packed = lax.optimization_barrier((low_edge, high_edge, packed))
+    packed = patch(packed, low_edge, high_edge)
+    packed, jac, op_main, op_mass = lax.optimization_barrier((packed, jac, op_main, op_mass))
     recv = lax.all_to_all(packed, "tm", 0, 0).reshape(LENGTH, BOX)
-    from_low = lax.ppermute(jac_top, "space", up)
-    from_high = lax.ppermute(jac_bottom, "space", down)
+    box = select_jac(jac)
     ops = select_ops(jnp.transpose(op_main, (1, 2, 0)), jnp.transpose(op_mass, (1, 2, 0)))
-    sent = solve(recv, ops, box, from_low, from_high)
+    sent = solve(recv, ops, box, low_edge, high_edge)
     back = lax.all_to_all(sent, "tm", 0, 0)
     return unpack(back)
 

time: 64 us -> 57.2 us (0.89)
  starting transfers between devices: 16.9 us -> 12.6 us
  waiting for transfers between devices: 0.01 us -> 3.72 us
  local copies, waits for them, and re-layouts: 4.31 us -> 1.05 us
  blocking collectives: 21.7 us -> 18.6 us
  Pallas kernels: 18.6 us -> 20.1 us
  other arithmetic: 0.96 us -> 0 us
    ppermute x2 -> x0, starting transfers between devices: 5.56 us -> none  [the longest x1 3.16 us: per_device(): from_low = lax.ppermute(jac_top, 'space', up)]
    all_to_all x1, waiting for transfers between devices: 0.01 us -> 3.71 us  [per_device(): recv = lax.all_to_all(packed, 'tm', 0, 0).reshape(LENGTH, BOX)]
    unnamed x10 -> x6, local copies, waits for them, and re-layouts: 4.31 us -> 1.05 us
    all_to_all x1, blocking collectives: 21.7 us -> 18.6 us  [per_device(): back = lax.all_to_all(sent, 'tm', 0, 0)]
    ppermute x1, starting transfers between devices: 1.92 us -> 3.64 us  [per_device(): high_edge = lax.ppermute(bottom, 'space', down)]
    pallas_call x1, Pallas kernels: 7.38 us -> 8.61 us  [select_ops(): pl.pallas_call(ops_kernel, grid=(BS // CHUNK,), in_specs=[spec, spec], ou...]
    convert_element_type x1 -> x0, other arithmetic: 0.95 us -> none  [per_device(): bottom = (forcing[:, :LAYER] * scale).astype(bf16)]
    pallas_call x3 -> x5, Pallas kernels: 8.92 us -> 9.22 us  [the longest x1 3.31 us: select_jac(): pl.pallas_call(jac_kernel, in_specs=[pl.BlockSpec(memory_space=pltpu.HBM)...]
  transfers between devices with their start and end apart: 5 -> 3, of which waited for: 0 -> 1; matrix products, arithmetic and copies ran while one was open for 0% -> 0% of each run, Pallas kernels for 19% -> 23%
where the time goes in v1:
time: 57.2 us; the launch traced here: 56.8 us
  Pallas kernels  20.1 us (35%)
  blocking collectives  18.6 us (33%)
  starting transfers between devices  12.6 us (22%)
  waiting for transfers between devices  3.72 us (7%)
  local copies, waits for them, and re-layouts  1.05 us (2%)
  between operations  0.74 us (1%)
    all_to_all x1, blocking collectives, per_device(): back = lax.all_to_all(sent, 'tm', 0, 0)  18.6 us
    pallas_call x1, Pallas kernels, select_ops(): pl.pallas_call(ops_kernel, grid=(BS // CHUNK,), in_specs=[spec, spec], ou...  8.61 us
    all_to_all x1, starting transfers between devices, per_device(): recv = lax.all_to_all(packed, 'tm', 0, 0).reshape(LENGTH, BOX)  7.05 us
    all_to_all x1, waiting for transfers between devices, per_device(): recv = lax.all_to_all(packed, 'tm', 0, 0).reshape(LENGTH, BOX)  3.71 us
    ppermute x1, starting transfers between devices, per_device(): high_edge = lax.ppermute(bottom, 'space', down)  3.64 us
    pallas_call x1, Pallas kernels, select_jac(): pl.pallas_call(jac_kernel, in_specs=[pl.BlockSpec(memory_space=pltpu.HBM)...  3.31 us
    pallas_call x1, Pallas kernels, edges(): pl.pallas_call(edge_kernel, in_specs=[hbm, hbm], out_shape=(edge, edge),...  2.46 us
    pallas_call x1, Pallas kernels, solve(): pl.pallas_call(solve_kernel, out_shape=jax.ShapeDtypeStruct((PARTS, 3 * S...  2.3 us
  transfers between devices with their start and end apart: 3, of which 1 were waited for; matrix products, arithmetic and copies ran while one was open for 0% of the time, Pallas kernels for 23%

profile of v1, /device:TPU:32, one launch (start us, length us, event | category | flops | bytes accessed | tf_op | source)
XLA Modules:
  0.0 56.8 jit_solution(1639064869475455846)
XLA Ops:
  0.6 2.5 %edges.1 = (bf16[32,1024]{1,0:T(8,128)(2,1)}, bf16[32,1024]{1,0:T(8,128)(2,1)}) custom-call(f32[16,8192]{1,0:T(8,128)} %source.1, bf16[64,64,128]{2,1,0:T(8,128)(2,1)} %bitcast.7), custom_call_target="tpu_custom_call" | custom-call | flops 100000000 | bytes 2000000 | tf_op jit(solution)/shard_map/edges/pallas_call | solution.py:234
  3.1 1.9 %collective-permute-start = (bf16[32,1024]{1,0:T(8,128)(2,1)}, bf16[32,1024]{1,0:T(8,128)(2,1)S(1)}, u32[]{:S(2)}, u32[]{:S(2)}) collective-permute-start(bf16[32,1024]{1,0:T(8,128)(2,1)} %get-tuple-element.12), channel_id=1, source_target_pairs={{0,1},{1,2},{2,3},{3,4},{4,5},{5,6},{6,7},{8,9},{9,10},{10,11},{11... | collective-permute-start | bytes 196616 | tf_op jit(solution)/shard_map/ppermute | solution.py:475
  5.0 3.6 %collective-permute-start.1 = (bf16[32,1024]{1,0:T(8,128)(2,1)}, bf16[32,1024]{1,0:T(8,128)(2,1)S(1)}, u32[]{:S(2)}, u32[]{:S(2)}) collective-permute-start(bf16[32,1024]{1,0:T(8,128)(2,1)} %get-tuple-element.13), channel_id=1, source_target_pairs={{1,0},{2,1},{3,2},{4,3},{5,4},{6,5},{7,6},{9,8},{10,9},{11,10},{12... | collective-permute-start | bytes 196616 | tf_op jit(solution)/shard_map/ppermute | solution.py:476
  8.7 0.0 copy-start
  8.7 1.0 %copy-done = f32[16,8192]{1,0:T(8,128)S(1)} copy-done((f32[16,8192]{1,0:T(8,128)S(1)}, f32[16,8192]{1,0:T(8,128)}, u32[]{:S(2)}) %copy-start) | copy-done | bytes 524312
  9.7 1.4 %pack.1.packed = bf16[16,16,1536]{2,1,0:T(8,128)(2,1)} custom-call(f32[16,8192]{1,0:T(8,128)S(1)} %copy-done), custom_call_target="tpu_custom_call" | custom-call | flops 1000000 | bytes 4000000 | tf_op jit(solution)/shard_map/pack/pallas_call | solution.py:112
  11.1 0.0 collective-permute-done.low_edge
  11.1 0.0 collective-permute-done.1.high_edge
  11.1 0.8 %patch.1 = bf16[16,16,1536]{2,1,0:T(8,128)(2,1)} custom-call(bf16[16,16,1536]{2,1,0:T(8,128)(2,1)} %pack.1.packed, bf16[32,1024]{1,0:T(8,128)(2,1)S(1)} %collective-permute-done.low_edge, bf16[32,1024]{1,0:T(8,128)(2,1)S(1)} %collective-permute-done.1.high_edge), custom_call_target="tpu_custom_call", output_to_operand_aliasing={{}: (0, {})} | custom-call | flops 1000 | bytes 200000 | tf_op jit(solution)/shard_map/patch/pallas_call | solution.py:146
  12.0 7.0 %all-to-all-start = ((bf16[16,16,1536]{2,1,0:T(8,128)(2,1)}), bf16[16,16,1536]{2,1,0:T(8,128)(2,1)S(1)}, u32[]{:S(2)}, u32[]{:S(2)}) async-start(bf16[16,16,1536]{2,1,0:T(8,128)(2,1)} %patch.1), calls=%async_computation | async-start | bytes 1572864 | tf_op jit(solution)/shard_map/all_to_all | solution.py:481
  19.0 3.3 %select_jac.1.box = bf16[64,1536]{1,0:T(8,128)(2,1)} custom-call(bf16[64,64,128]{2,1,0:T(8,128)(2,1)} %bitcast.8), custom_call_target="tpu_custom_call" | custom-call | flops 1000000000 | bytes 2000000 | tf_op jit(solution)/shard_map/select_jac/pallas_call | solution.py:271
  22.3 0.0 copy-start.1
  22.4 0.0 copy-start.2
  22.4 8.6 %select_ops.1.ops = bf16[4,768,256]{2,1,0:T(8,128)(2,1)S(1)} custom-call(bf16[64,448,128]{2,1,0:T(8,128)(2,1)} %bitcast.5, bf16[64,448,128]{2,1,0:T(8,128)(2,1)} %bitcast.6), custom_call_target="tpu_custom_call" | custom-call | flops 4000000000 | bytes 16000000 | tf_op jit(solution)/shard_map/select_ops/pallas_call | solution.py:340
  31.0 3.7 %all-to-all-done = bf16[16,16,1536]{2,1,0:T(8,128)(2,1)S(1)} async-done(((bf16[16,16,1536]{2,1,0:T(8,128)(2,1)}), bf16[16,16,1536]{2,1,0:T(8,128)(2,1)S(1)}, u32[]{:S(2)}, u32[]{:S(2)}) %all-to-all-start) | async-done | bytes 786464 | tf_op jit(solution)/shard_map/all_to_all | solution.py:481
  34.7 0.0 copy-done.1
  34.7 0.0 copy-done.2
  34.7 2.3 %solve.1 = bf16[16,48,512]{2,1,0:T(8,128)(2,1)S(1)} custom-call(bf16[256,1536]{1,0:T(8,128)(2,1)S(1)} %bitcast.4, bf16[4,768,256]{2,1,0:T(8,128)(2,1)S(1)} %select_ops.1.ops, bf16[64,1536]{1,0:T(8,128)(2,1)S(1)} %copy-done.2, bf16[32,1024]{1,0:T(8,128)(2,1)S(1)} %collective-permute-done.low_edge, bf16[32,1024]{1,0:T(8,128)(2,1)S(1)} %collective-permute-done.1.high_edge, ...), custom_call_target="tpu_custom_call" | custom-call | flops 3000000000 | bytes 5000000 | tf_op jit(solution)/shard_map/solve/pallas_call | solution.py:421
  37.0 18.6 %all_to_all.10.recv = bf16[16,48,512]{2,1,0:T(8,128)(2,1)S(1)} all-to-all(bf16[16,48,512]{2,1,0:T(8,128)(2,1)S(1)} %solve.1), channel_id=1, replica_groups=mesh['tm'=16,'space'=8] {'tm'}, dimensions={0} | all-to-all | bytes 1572864 | tf_op jit(solution)/shard_map/all_to_all | solution.py:485
  55.6 1.2 %unpack.1 = (f32[16,8192]{1,0:T(8,128)}, f32[16,8192]{1,0:T(8,128)}, f32[16,8192]{1,0:T(8,128)}) custom-call(bf16[16,48,512]{2,1,0:T(8,128)(2,1)S(1)} %all_to_all.10.recv), custom_call_target="tpu_custom_call" | custom-call | flops 1000000 | bytes 3000000 | tf_op jit(solution)/shard_map/unpack/pallas_call | solution.py:458
Async XLA Ops:
  3.1 8.0 %collective-permute-start = (bf16[32,1024]{1,0:T(8,128)(2,1)}, bf16[32,1024]{1,0:T(8,128)(2,1)S(1)}, u32[]{:S(2)}, u32[]{:S(2)}) collective-permute-start(bf16[32,1024]{1,0:T(8,128)(2,1)} %get-tuple-element.12), channel_id=1, source_target_pairs={{0,1},{1,2},{2,3},{3,4},{4,5},{5,6},{6,7},{8,9},{9,10},{10,11},{11... | collective-permute-start | bytes 196616 | tf_op jit(solution)/shard_map/ppermute | solution.py:475
  5.0 6.1 %collective-permute-start.1 = (bf16[32,1024]{1,0:T(8,128)(2,1)}, bf16[32,1024]{1,0:T(8,128)(2,1)S(1)}, u32[]{:S(2)}, u32[]{:S(2)}) collective-permute-start(bf16[32,1024]{1,0:T(8,128)(2,1)} %get-tuple-element.13), channel_id=1, source_target_pairs={{1,0},{2,1},{3,2},{4,3},{5,4},{6,5},{7,6},{9,8},{10,9},{11,10},{12... | collective-permute-start | bytes 196616 | tf_op jit(solution)/shard_map/ppermute | solution.py:476
  8.7 1.0 %copy-start = (f32[16,8192]{1,0:T(8,128)S(1)}, f32[16,8192]{1,0:T(8,128)}, u32[]{:S(2)}) copy-start(f32[16,8192]{1,0:T(8,128)} %source.1) | copy-start | bytes 1572868
  12.0 22.7 %all-to-all-start = ((bf16[16,16,1536]{2,1,0:T(8,128)(2,1)}), bf16[16,16,1536]{2,1,0:T(8,128)(2,1)S(1)}, u32[]{:S(2)}, u32[]{:S(2)}) async-start(bf16[16,16,1536]{2,1,0:T(8,128)(2,1)} %patch.1), calls=%async_computation | async-start | bytes 1572864 | tf_op jit(solution)/shard_map/all_to_all | solution.py:481
  22.3 12.4 %copy-start.1 = (bf16[512,768]{1,0:T(8,128)(2,1)S(1)}, bf16[512,768]{1,0:T(8,128)(2,1)}, u32[]{:S(2)}) copy-start(bf16[512,768]{1,0:T(8,128)(2,1)} %constant.2.clone.table) | copy-start | bytes 2359300
  22.4 12.3 %copy-start.2 = (bf16[64,1536]{1,0:T(8,128)(2,1)S(1)}, bf16[64,1536]{1,0:T(8,128)(2,1)}, u32[]{:S(2)}) copy-start(bf16[64,1536]{1,0:T(8,128)(2,1)} %select_jac.1.box) | copy-start | bytes 589828

commit v2 on v1

--- a/solution.py
+++ b/solution.py
@@ -120,28 +120,39 @@
     )(forcing)
 
 
-def patch_kernel(packed, low_edge, high_edge, out, sems):
-    copies = []
-    for dest in range(PARTS):
-        zg, yg, xg = box_of(dest)
-        for edge, at_group, first in ((low_edge, 0, 4), (high_edge, 3, 6)):
-            if zg == at_group:
-                for d in range(2):
-                    at = (2 * yg + d) * ROW + xg * COL
-                    copies.append(
-                        pltpu.make_async_copy(
-                            edge.at[pl.ds(0, STEPS), pl.ds(at, COL)],
-                            out.at[dest, :, pl.ds((first + d) * COL, COL)],
-                            sems.at[len(copies)],
+def patch_kernel(packed, near, far, out, sems):
+    def place(low_edge, high_edge):
+        copies = []
+        for dest in range(PARTS):
+            zg, yg, xg = box_of(dest)
+            for edge, at_group, first in ((low_edge, 0, 4), (high_edge, 3, 6)):
+                if zg == at_group:
+                    for d in range(2):
+                        at = (2 * yg + d) * ROW + xg * COL
+                        copies.append(
+                            pltpu.make_async_copy(
+                                edge.at[pl.ds(0, STEPS), pl.ds(at, COL)],
+                                out.at[dest, :, pl.ds((first + d) * COL, COL)],
+                                sems.at[len(copies)],
+                            )
                         )
-                    )
-    for copy in copies:
-        copy.start()
-    for copy in copies:
-        copy.wait()
-
-
-def patch(packed, low_edge, high_edge):
+        for copy in copies:
+            copy.start()
+        for copy in copies:
+            copy.wait()
+
+    core = lax.axis_index("space") % 2
+
+    @pl.when(core == 0)
+    def _():
+        place(far, near)
+
+    @pl.when(core == 1)
+    def _():
+        place(near, far)
+
+
+def patch(packed, near, far):
     anywhere = pl.BlockSpec(memory_space=pl.ANY)
     return pl.pallas_call(
         patch_kernel,
@@ -153,7 +164,7 @@
         name="patch",
         compiler_params=pltpu.CompilerParams(vmem_limit_bytes=2**20),
         cost_estimate=cost(10**3, 2 * 10**5),
-    )(packed, low_edge, high_edge)
+    )(packed, near, far)
 
 
 def selector(blocks, width):
@@ -201,31 +212,34 @@
     return z * 16 + y * 4 + x
 
 
-def edge_kernel(forcing, jac, top, bottom, ends, local, sems):
+def edge_kernel(forcing, jac, near, far, ends, local, sems):
+    _, yg, xg = box_of(lax.axis_index("tm"))
+    near_layer = jnp.where(lax.axis_index("space") % 2 == 0, LAYERS - 1, 0)
     copies = [
-        pltpu.make_async_copy(jac, local, sems.at[0]),
-        pltpu.make_async_copy(forcing.at[:, pl.ds(0, LAYER)], ends.at[0], sems.at[1]),
         pltpu.make_async_copy(
-            forcing.at[:, pl.ds(SLAB - LAYER, LAYER)], ends.at[1], sems.at[2]
-        ),
+            forcing.at[:, pl.ds(pl.multiple_of(layer * LAYER, LAYER), LAYER)],
+            ends.at[which],
+            sems.at[which],
+        )
+        for which, layer in enumerate((near_layer, LAYERS - 1 - near_layer))
     ]
+    copies.append(pltpu.make_async_copy(jac, local, sems.at[2]))
     for copy in copies:
         copy.start()
-    _, yg, xg = box_of(lax.axis_index("tm"))
     scale = jnp.concatenate([scales()] * (LAYER // COL), axis=1)
     slot = slots_of()
-    layer = jnp.where(slot < 4, LAYERS - 1, 0)
+    layer = jnp.where(slot < 4, near_layer, LAYERS - 1 - near_layer)
     blocks = block_at(layer, 2 * yg + slot // 2 % 2, 2 * xg + slot % 2)
     perm = reorder(4 * COL)
-    for copy in copies:
-        copy.wait()
-    bottom[:STEPS] = (ends[0] * scale).astype(bf16)
-    top[:STEPS] = (ends[1] * scale).astype(bf16)
+    for which, out in enumerate((near, far)):
+        copies[which].wait()
+        out[:STEPS] = (ends[which] * scale).astype(bf16)
+    copies[2].wait()
     picked = select_all(local, blocks, perm)
     for a in range(BS // STEPS):
         cut = slice(a * 2 * COL, (a + 1) * 2 * COL)
-        top[STEPS:, cut] = picked[a * STEPS : (a + 1) * STEPS, : 2 * COL]
-        bottom[STEPS:, cut] = picked[a * STEPS : (a + 1) * STEPS, 2 * COL :]
+        near[STEPS:, cut] = picked[a * STEPS : (a + 1) * STEPS, : 2 * COL]
+        far[STEPS:, cut] = picked[a * STEPS : (a + 1) * STEPS, 2 * COL :]
 
 
 def edges(forcing, jac):
@@ -246,7 +260,7 @@
     )(forcing, jac)
 
 
-def jac_kernel(jac, box, local, sem):
+def jac_kernel(jac, near, far, box, local, sem):
     copy = pltpu.make_async_copy(jac, local, sem)
     copy.start()
     zg, yg, xg = box_of(lax.axis_index("tm"))
@@ -263,20 +277,36 @@
     ahead = block_at(2 * zg + d, 2 * yg + e, 2 - xg)
     perm = reorder(4 * COL)
     copy.wait()
+    even = lax.axis_index("space") % 2 == 0
+
+    def other(edge):
+        pieces = [edge[STEPS:, 2 * a * COL : 2 * (a + 1) * COL] for a in range(BS // STEPS)]
+        return jnp.concatenate(pieces, axis=0)
+
+    near, far = other(near), other(far)
     for at, blocks in enumerate((own, faces, jnp.where(first, beside, ahead))):
-        box[:, at * 4 * COL : (at + 1) * 4 * COL] = select_all(local, blocks, perm)
-
-
-def select_jac(jac):
+        both = select_all(local, blocks, perm)
+        for which in range(2):
+            value = both[:, which * 2 * COL : (which + 1) * 2 * COL]
+            if at == 1 and which == 0:
+                value = jnp.where(zg == 0, jnp.where(even, far, near), value)
+            if at == 1 and which == 1:
+                value = jnp.where(zg == 3, jnp.where(even, near, far), value)
+            p = 2 * at + which
+            box[:, 2 * p * COL : 2 * (p + 1) * COL] = value
+
+
+def select_jac(jac, near, far):
+    vmem = pl.BlockSpec(memory_space=pltpu.VMEM)
     return pl.pallas_call(
         jac_kernel,
-        in_specs=[pl.BlockSpec(memory_space=pltpu.HBM)],
+        in_specs=[pl.BlockSpec(memory_space=pltpu.HBM), vmem, vmem],
         out_shape=jax.ShapeDtypeStruct((BS, BOX), bf16),
         scratch_shapes=[pltpu.VMEM((BS, BS, BLOCKS), bf16), pltpu.SemaphoreType.DMA],
         name="select_jac",
-        compiler_params=pltpu.CompilerParams(vmem_limit_bytes=63 * 10**6),
+        compiler_params=pltpu.CompilerParams(vmem_limit_bytes=8 * 2**20),
         cost_estimate=cost(10**9, 2 * 10**6),
-    )(jac)
+    )(jac, near, far)
 
 
 def ops_kernel(main, mass, out, chosen, picked):
@@ -353,39 +383,29 @@
     )(main, mass)
 
 
-def solve_kernel(recv, ops, box, low_edge, high_edge, table, out):
-    zg, _, _ = box_of(lax.axis_index("tm"))
-    low = lax.broadcasted_iota(jnp.int32, (BS, COL), 1) < BS
-    zero = jnp.zeros((BS, COL), bf16)
-
-    def fields(c):
-        return recv[:, c * COL : (c + 1) * COL]
-
-    def other(edge, d):
-        pieces = [
-            edge[STEPS:, (2 * a + d) * COL : (2 * a + d + 1) * COL] for a in range(BS // STEPS)
-        ]
-        return jnp.concatenate(pieces, axis=0)
-
-    def inverse(c):
-        value = box[:, c * COL : (c + 1) * COL]
-        if c in (4, 5):
-            value = jnp.where(zg == 0, other(low_edge, c - 4), value)
-        if c in (6, 7):
-            value = jnp.where(zg == 3, other(high_edge, c - 6), value)
-        return jnp.concatenate(
-            [jnp.where(low, value, zero), jnp.where(low, zero, value)], axis=0
-        )
-
-    inverses = [inverse(c) for c in range(4)]
-    firsts = [dot(fields(c), inverses[c]) for c in range(4)]
-    lows = [value.astype(bf16) for value in firsts]
-    lows += [dot(fields(c), inverse(c)).astype(bf16) for c in range(4, 12)]
-
-    ids = step_ids(0, LENGTH, COL).astype(f32)
+def solve_kernel(recv, ops, box, table, out):
+    lane = lax.broadcasted_iota(jnp.int32, (BS, 2 * COL), 1) // BS
+
+    def diagonal(p):
+        value = box[:, 2 * p * COL : 2 * (p + 1) * COL]
+        rows = [jnp.where(lane == q, value, jnp.zeros_like(value)) for q in range(4)]
+        return jnp.concatenate(rows, axis=0)
+
+    diagonals = [diagonal(p) for p in range(6)]
+
+    def fields(c, count):
+        return recv[:, c * COL : (c + count) * COL]
+
+    firsts = [dot(fields(2 * p, 2), diagonals[p]) for p in range(2)]
+    halves = [value.astype(bf16) for value in firsts]
+    halves += [dot(fields(2 * p, 2), diagonals[p]).astype(bf16) for p in range(2, 6)]
+    lows = [half[:, e * COL : (e + 1) * COL] for half in halves for e in range(2)]
+
+    ids = step_ids(0, LENGTH, 2 * COL).astype(f32)
     growth = jnp.exp(ids * -LOG_STEP)
     seconds = []
     for dz in range(2):
+        residues = []
         for dy in range(2):
             pair = 2 * dz + dy
             around = jnp.concatenate(
@@ -401,14 +421,15 @@
             )
             image = dot(around, ops[pair])
             earlier = pltpu.roll(image[:, COL:], 1, 0)
-            residue = fields(pair).astype(f32) - image[:, :COL] + MODULUS * earlier
-            second = firsts[pair] + dot(residue.astype(bf16), inverses[pair])
-            in_time = (second * growth).astype(bf16)
-            for dest in range(PARTS):
-                out[dest, 2 * STEPS :, pair * COL : (pair + 1) * COL] = in_time[
-                    dest * STEPS : (dest + 1) * STEPS
-                ]
-            seconds.append(second)
+            residue = fields(pair, 1).astype(f32) - image[:, :COL] + MODULUS * earlier
+            residues.append(residue.astype(bf16))
+        second = firsts[dz] + dot(jnp.concatenate(residues, axis=1), diagonals[dz])
+        in_time = (second * growth).astype(bf16)
+        for dest in range(PARTS):
+            out[dest, 2 * STEPS :, 2 * dz * COL : 2 * (dz + 1) * COL] = in_time[
+                dest * STEPS : (dest + 1) * STEPS
+            ]
+        seconds.append(second)
     second = jnp.concatenate(seconds, axis=1)
     high = second.astype(bf16)
     rest = (second - high.astype(f32)).astype(bf16)
@@ -417,14 +438,14 @@
         out[dest, : 2 * STEPS] = spectrum[dest * 2 * STEPS : (dest + 1) * 2 * STEPS]
 
 
-def solve(recv, ops, box, low_edge, high_edge):
+def solve(recv, ops, box):
     return pl.pallas_call(
         solve_kernel,
         out_shape=jax.ShapeDtypeStruct((PARTS, 3 * STEPS, OWN), bf16),
         name="solve",
-        compiler_params=pltpu.CompilerParams(vmem_limit_bytes=40 * 2**20),
+        compiler_params=pltpu.CompilerParams(vmem_limit_bytes=16 * 2**20),
         cost_estimate=cost(3 * 10**9, 5 * 10**6),
-    )(recv, ops, box, low_edge, high_edge, jnp.asarray(dft_table()))
+    )(recv, ops, box, jnp.asarray(dft_table()))
 
 
 def unpack_kernel(recv, real, imag, in_time, ready, sems):
@@ -468,20 +489,23 @@
 
 def per_device(forcing, op_main, op_mass, jacobi_inv):
     count = lax.axis_size("space")
-    up = [(i, i + 1) for i in range(count - 1)]
-    down = [(i + 1, i) for i in range(count - 1)]
+    across = [(i, i + 1) for i in range(1, count - 1, 2)]
+    within = [(i, i + 1) for i in range(0, count, 2)]
+    across += [(j, i) for i, j in across]
+    within += [(j, i) for i, j in within]
     jac = jnp.transpose(jacobi_inv, (1, 2, 0))
-    top, bottom = edges(forcing, jac)
-    low_edge = lax.ppermute(top, "space", up)
-    high_edge = lax.ppermute(bottom, "space", down)
+    near, far = edges(forcing, jac)
+    far = lax.ppermute(far, "space", across)
+    near = lax.ppermute(near, "space", within)
     packed = pack(forcing)
-    low_edge, high_edge, packed = lax.optimization_barrier((low_edge, high_edge, packed))
-    packed = patch(packed, low_edge, high_edge)
-    packed, jac, op_main, op_mass = lax.optimization_barrier((packed, jac, op_main, op_mass))
+    near, far, packed = lax.optimization_barrier((near, far, packed))
+    packed = patch(packed, near, far)
+    packed, op_main, op_mass = lax.optimization_barrier((packed, op_main, op_mass))
     recv = lax.all_to_all(packed, "tm", 0, 0).reshape(LENGTH, BOX)
-    box = select_jac(jac)
     ops = select_ops(jnp.transpose(op_main, (1, 2, 0)), jnp.transpose(op_mass, (1, 2, 0)))
-    sent = solve(recv, ops, box, low_edge, high_edge)
+    ops, jac = lax.optimization_barrier((ops, jac))
+    box = select_jac(jac, near, far)
+    sent = solve(recv, ops, box)
     back = lax.all_to_all(sent, "tm", 0, 0)
     return unpack(back)
 

time: 57.2 us -> 52.6 us (0.920)
  starting transfers between devices: 12.6 us -> 9.16 us
  waiting for transfers between devices: 3.72 us -> 6.42 us
  Pallas kernels: 20.1 us -> 18 us
  blocking collectives: 18.6 us -> 16.9 us
    ppermute x2, starting transfers between devices: 5.56 us -> 2.11 us  [the longest x1 2.02 us: per_device(): far = lax.ppermute(far, 'space', across)]
    pallas_call x1, Pallas kernels: 3.31 us -> 1.63 us  [select_jac(): pl.pallas_call(jac_kernel, in_specs=[pl.BlockSpec(memory_space=pltpu.HBM)...]
    all_to_all x1, blocking collectives: 18.6 us -> 16.9 us  [per_device(): back = lax.all_to_all(sent, 'tm', 0, 0)]
    all_to_all x1, waiting for transfers between devices: 3.71 us -> 5.11 us  [per_device(): recv = lax.all_to_all(packed, 'tm', 0, 0).reshape(LENGTH, BOX)]
    ppermute x2, waiting for transfers between devices: 0.01 us -> 1.31 us  [the longest x1 1.31 us: per_device(): far = lax.ppermute(far, 'space', across)]
    pallas_call x1, Pallas kernels: 2.3 us -> 1.68 us  [solve(): pl.pallas_call(solve_kernel, out_shape=jax.ShapeDtypeStruct((PARTS, 3 * S...]
  transfers between devices with their start and end apart: 3 -> 3, of which waited for: 1 -> 2; matrix products, arithmetic and copies ran while one was open for 0% -> 0% of each run, Pallas kernels for 23% -> 22%
where the time goes in v2:
time: 52.6 us; the launch traced here: 52.3 us
  Pallas kernels  18 us (34%)
  blocking collectives  16.9 us (32%)
  starting transfers between devices  9.16 us (17%)
  waiting for transfers between devices  6.42 us (12%)
  local copies, waits for them, and re-layouts  1.05 us (2%)
  between operations  0.74 us (1%)
    all_to_all x1, blocking collectives, per_device(): back = lax.all_to_all(sent, 'tm', 0, 0)  16.9 us
    pallas_call x1, Pallas kernels, select_ops(): pl.pallas_call(ops_kernel, grid=(BS // CHUNK,), in_specs=[spec, spec], ou...  8.66 us
    all_to_all x1, starting transfers between devices, per_device(): recv = lax.all_to_all(packed, 'tm', 0, 0).reshape(LENGTH, BOX)  7.05 us
    all_to_all x1, waiting for transfers between devices, per_device(): recv = lax.all_to_all(packed, 'tm', 0, 0).reshape(LENGTH, BOX)  5.11 us
    pallas_call x1, Pallas kernels, edges(): pl.pallas_call(edge_kernel, in_specs=[hbm, hbm], out_shape=(edge, edge),...  2.55 us
    ppermute x1, starting transfers between devices, per_device(): far = lax.ppermute(far, 'space', across)  2.02 us
    pallas_call x1, Pallas kernels, solve(): pl.pallas_call(solve_kernel, out_shape=jax.ShapeDtypeStruct((PARTS, 3 * S...  1.68 us
    pallas_call x1, Pallas kernels, select_jac(): pl.pallas_call(jac_kernel, in_specs=[pl.BlockSpec(memory_space=pltpu.HBM)...  1.63 us
  transfers between devices with their start and end apart: 3, of which 2 were waited for; matrix products, arithmetic and copies ran while one was open for 0% of the time, Pallas kernels for 22%

profile of v2, /device:TPU:32, one launch (start us, length us, event | category | flops | bytes accessed | tf_op | source)
XLA Modules:
  0.0 52.3 jit_solution(8514391003103218674)
XLA Ops:
  0.6 2.5 %edges.1 = (bf16[32,1024]{1,0:T(8,128)(2,1)}, bf16[32,1024]{1,0:T(8,128)(2,1)}) custom-call(f32[16,8192]{1,0:T(8,128)} %source.1, bf16[64,64,128]{2,1,0:T(8,128)(2,1)} %bitcast.4), custom_call_target="tpu_custom_call" | custom-call | flops 100000000 | bytes 2000000 | tf_op jit(solution)/shard_map/edges/pallas_call | solution.py:248
  3.2 0.1 collective-permute-start
  3.3 2.0 %collective-permute-start.1 = (bf16[32,1024]{1,0:T(8,128)(2,1)}, bf16[32,1024]{1,0:T(8,128)(2,1)S(1)}, u32[]{:S(2)}, u32[]{:S(2)}) collective-permute-start(bf16[32,1024]{1,0:T(8,128)(2,1)} %get-tuple-element.14), channel_id=1, source_target_pairs={{1,2},{3,4},{5,6},{2,1},{4,3},{6,5},{9,10},{11,12},{13,14},{10,9},... | collective-permute-start | bytes 196616 | tf_op jit(solution)/shard_map/ppermute | solution.py:498
  5.3 0.0 copy-start
  5.3 1.0 %copy-done = f32[16,8192]{1,0:T(8,128)S(1)} copy-done((f32[16,8192]{1,0:T(8,128)S(1)}, f32[16,8192]{1,0:T(8,128)}, u32[]{:S(2)}) %copy-start) | copy-done | bytes 524312
  6.4 1.4 %pack.1.packed = bf16[16,16,1536]{2,1,0:T(8,128)(2,1)} custom-call(f32[16,8192]{1,0:T(8,128)S(1)} %copy-done), custom_call_target="tpu_custom_call" | custom-call | flops 1000000 | bytes 4000000 | tf_op jit(solution)/shard_map/pack/pallas_call | solution.py:112
  7.8 0.0 collective-permute-done.near
  7.8 1.3 %collective-permute-done.1.far = bf16[32,1024]{1,0:T(8,128)(2,1)S(1)} collective-permute-done((bf16[32,1024]{1,0:T(8,128)(2,1)}, bf16[32,1024]{1,0:T(8,128)(2,1)S(1)}, u32[]{:S(2)}, u32[]{:S(2)}) %collective-permute-start.1) | collective-permute-done | bytes 65568 | tf_op jit(solution)/shard_map/ppermute | solution.py:498
  9.1 0.8 %patch.1 = bf16[16,16,1536]{2,1,0:T(8,128)(2,1)} custom-call(bf16[16,16,1536]{2,1,0:T(8,128)(2,1)} %pack.1.packed, bf16[32,1024]{1,0:T(8,128)(2,1)S(1)} %collective-permute-done.near, bf16[32,1024]{1,0:T(8,128)(2,1)S(1)} %collective-permute-done.1.far), custom_call_target="tpu_custom_call", output_to_operand_aliasing={{}: (0, {})} | custom-call | flops 1000 | bytes 200000 | tf_op jit(solution)/shard_map/patch/pallas_call | solution.py:157
  9.9 7.0 %all-to-all-start = ((bf16[16,16,1536]{2,1,0:T(8,128)(2,1)}), bf16[16,16,1536]{2,1,0:T(8,128)(2,1)S(1)}, u32[]{:S(2)}, u32[]{:S(2)}) async-start(bf16[16,16,1536]{2,1,0:T(8,128)(2,1)} %patch.1), calls=%async_computation | async-start | bytes 1572864 | tf_op jit(solution)/shard_map/all_to_all | solution.py:504
  17.0 0.0 copy-start.1
  17.0 0.0 copy-start.2
  17.0 8.7 %select_ops.1.ops = bf16[4,768,256]{2,1,0:T(8,128)(2,1)S(1)} custom-call(bf16[64,448,128]{2,1,0:T(8,128)(2,1)} %bitcast.7, bf16[64,448,128]{2,1,0:T(8,128)(2,1)} %bitcast.8), custom_call_target="tpu_custom_call" | custom-call | flops 4000000000 | bytes 16000000 | tf_op jit(solution)/shard_map/select_ops/pallas_call | solution.py:370
  25.7 0.0 copy-done.1
  25.7 1.6 %select_jac.1.box = bf16[64,1536]{1,0:T(8,128)(2,1)S(1)} custom-call(bf16[64,64,128]{2,1,0:T(8,128)(2,1)S(1)} %bitcast.5, bf16[32,1024]{1,0:T(8,128)(2,1)S(1)} %collective-permute-done.near, bf16[32,1024]{1,0:T(8,128)(2,1)S(1)} %collective-permute-done.1.far), custom_call_target="tpu_custom_call" | custom-call | flops 1000000000 | bytes 2000000 | tf_op jit(solution)/shard_map/select_jac/pallas_call | solution.py:301
  27.3 5.1 %all-to-all-done = bf16[16,16,1536]{2,1,0:T(8,128)(2,1)S(1)} async-done(((bf16[16,16,1536]{2,1,0:T(8,128)(2,1)}), bf16[16,16,1536]{2,1,0:T(8,128)(2,1)S(1)}, u32[]{:S(2)}, u32[]{:S(2)}) %all-to-all-start) | async-done | bytes 786464 | tf_op jit(solution)/shard_map/all_to_all | solution.py:504
  32.4 0.0 copy-done.2
  32.4 1.7 %solve.1 = bf16[16,48,512]{2,1,0:T(8,128)(2,1)S(1)} custom-call(bf16[256,1536]{1,0:T(8,128)(2,1)S(1)} %bitcast.6, bf16[4,768,256]{2,1,0:T(8,128)(2,1)S(1)} %select_ops.1.ops, bf16[64,1536]{1,0:T(8,128)(2,1)S(1)} %select_jac.1.box, bf16[512,768]{1,0:T(8,128)(2,1)S(1)} %copy-done.2), custom_call_target="tpu_custom_call" | custom-call | flops 3000000000 | bytes 5000000 | tf_op jit(solution)/shard_map/solve/pallas_call | solution.py:442
  34.1 16.9 %all_to_all.10.recv = bf16[16,48,512]{2,1,0:T(8,128)(2,1)S(1)} all-to-all(bf16[16,48,512]{2,1,0:T(8,128)(2,1)S(1)} %solve.1), channel_id=1, replica_groups=mesh['tm'=16,'space'=8] {'tm'}, dimensions={0} | all-to-all | bytes 1572864 | tf_op jit(solution)/shard_map/all_to_all | solution.py:509
  51.1 1.2 %unpack.1 = (f32[16,8192]{1,0:T(8,128)}, f32[16,8192]{1,0:T(8,128)}, f32[16,8192]{1,0:T(8,128)}) custom-call(bf16[16,48,512]{2,1,0:T(8,128)(2,1)S(1)} %all_to_all.10.recv), custom_call_target="tpu_custom_call" | custom-call | flops 1000000 | bytes 3000000 | tf_op jit(solution)/shard_map/unpack/pallas_call | solution.py:479
Async XLA Ops:
  3.2 4.6 %collective-permute-start = (bf16[32,1024]{1,0:T(8,128)(2,1)}, bf16[32,1024]{1,0:T(8,128)(2,1)S(1)}, u32[]{:S(2)}, u32[]{:S(2)}) collective-permute-start(bf16[32,1024]{1,0:T(8,128)(2,1)} %get-tuple-element.13), channel_id=1, source_target_pairs={{0,1},{2,3},{4,5},{6,7},{1,0},{3,2},{5,4},{7,6},{8,9},{10,11},{12,... | collective-permute-start | bytes 196616 | tf_op jit(solution)/shard_map/ppermute | solution.py:499
  3.3 5.8 %collective-permute-start.1 = (bf16[32,1024]{1,0:T(8,128)(2,1)}, bf16[32,1024]{1,0:T(8,128)(2,1)S(1)}, u32[]{:S(2)}, u32[]{:S(2)}) collective-permute-start(bf16[32,1024]{1,0:T(8,128)(2,1)} %get-tuple-element.14), channel_id=1, source_target_pairs={{1,2},{3,4},{5,6},{2,1},{4,3},{6,5},{9,10},{11,12},{13,14},{10,9},... | collective-permute-start | bytes 196616 | tf_op jit(solution)/shard_map/ppermute | solution.py:498
  5.3 1.0 %copy-start = (f32[16,8192]{1,0:T(8,128)S(1)}, f32[16,8192]{1,0:T(8,128)}, u32[]{:S(2)}) copy-start(f32[16,8192]{1,0:T(8,128)} %source.1) | copy-start | bytes 1572868
  9.9 22.5 %all-to-all-start = ((bf16[16,16,1536]{2,1,0:T(8,128)(2,1)}), bf16[16,16,1536]{2,1,0:T(8,128)(2,1)S(1)}, u32[]{:S(2)}, u32[]{:S(2)}) async-start(bf16[16,16,1536]{2,1,0:T(8,128)(2,1)} %patch.1), calls=%async_computation | async-start | bytes 1572864 | tf_op jit(solution)/shard_map/all_to_all | solution.py:504
  17.0 8.7 %copy-start.1 = (bf16[128,64,64]{0,2,1:T(8,128)(2,1)S(1)}, bf16[128,64,64]{0,2,1:T(8,128)(2,1)}, u32[]{:S(2)}) copy-start(bf16[128,64,64]{0,2,1:T(8,128)(2,1)} %param.8) | copy-start | bytes 3145732
  17.0 15.4 %copy-start.2 = (bf16[512,768]{1,0:T(8,128)(2,1)S(1)}, bf16[512,768]{1,0:T(8,128)(2,1)}, u32[]{:S(2)}) copy-start(bf16[512,768]{1,0:T(8,128)(2,1)} %constant.2.clone.table) | copy-start | bytes 2359300

commit v3 on v2

--- a/solution.py
+++ b/solution.py
@@ -66,17 +66,7 @@
     return jnp.exp(ids * LOG_STEP)
 
 
-def pack_kernel(source, out, forcing, sems):
-    copies = []
-    for group in range(4):
-        cut = pl.ds(group * 2 * LAYER, 2 * LAYER)
-        copies.append(
-            pltpu.make_async_copy(source.at[:, cut], forcing.at[:, cut], sems.at[group])
-        )
-    for copy in copies:
-        copy.start()
-    for copy in copies:
-        copy.wait()
+def pack_kernel(forcing, out):
     scale = scales()
     half = lax.broadcasted_iota(jnp.int32, (STEPS, COL), 1) < BS
 
@@ -111,16 +101,15 @@
 def pack(forcing):
     return pl.pallas_call(
         pack_kernel,
-        in_specs=[pl.BlockSpec(memory_space=pltpu.HBM)],
+        in_specs=[pl.BlockSpec(memory_space=pltpu.VMEM)],
         out_shape=jax.ShapeDtypeStruct((PARTS, STEPS, BOX), bf16),
-        scratch_shapes=[pltpu.VMEM((STEPS, SLAB), f32), pltpu.SemaphoreType.DMA((4,))],
         name="pack",
         compiler_params=pltpu.CompilerParams(vmem_limit_bytes=6 * 2**20),
         cost_estimate=cost(10**6, 4 * 10**6),
     )(forcing)
 
 
-def patch_kernel(packed, near, far, out, sems):
+def patch_kernel(packed, far, near, out, sems):
     def place(low_edge, high_edge):
         copies = []
         for dest in range(PARTS):
@@ -152,7 +141,7 @@
         place(near, far)
 
 
-def patch(packed, near, far):
+def patch(packed, far, near):
     anywhere = pl.BlockSpec(memory_space=pl.ANY)
     return pl.pallas_call(
         patch_kernel,
@@ -164,7 +153,7 @@
         name="patch",
         compiler_params=pltpu.CompilerParams(vmem_limit_bytes=2**20),
         cost_estimate=cost(10**3, 2 * 10**5),
-    )(packed, near, far)
+    )(packed, far, near)
 
 
 def selector(blocks, width):
@@ -212,34 +201,37 @@
     return z * 16 + y * 4 + x
 
 
-def edge_kernel(forcing, jac, near, far, ends, local, sems):
+def edge_kernel(forcing, jac, far, near, held, local, sems):
     _, yg, xg = box_of(lax.axis_index("tm"))
     near_layer = jnp.where(lax.axis_index("space") % 2 == 0, LAYERS - 1, 0)
+    first, middle, last = LAYER, SLAB - 2 * LAYER, LAYER
+    cuts = [pl.ds(0, first), pl.ds(SLAB - last, last), pl.ds(first, middle)]
     copies = [
-        pltpu.make_async_copy(
-            forcing.at[:, pl.ds(pl.multiple_of(layer * LAYER, LAYER), LAYER)],
-            ends.at[which],
-            sems.at[which],
-        )
-        for which, layer in enumerate((near_layer, LAYERS - 1 - near_layer))
+        pltpu.make_async_copy(forcing.at[:, cut], held.at[:, cut], sems.at[which])
+        for which, cut in enumerate(cuts)
     ]
-    copies.append(pltpu.make_async_copy(jac, local, sems.at[2]))
-    for copy in copies:
-        copy.start()
+    copies.append(pltpu.make_async_copy(jac, local, sems.at[3]))
+    for which in (0, 1, 3, 2):
+        copies[which].start()
     scale = jnp.concatenate([scales()] * (LAYER // COL), axis=1)
     slot = slots_of()
     layer = jnp.where(slot < 4, near_layer, LAYERS - 1 - near_layer)
     blocks = block_at(layer, 2 * yg + slot // 2 % 2, 2 * xg + slot % 2)
     perm = reorder(4 * COL)
-    for which, out in enumerate((near, far)):
-        copies[which].wait()
-        out[:STEPS] = (ends[which] * scale).astype(bf16)
-    copies[2].wait()
+    copies[0].wait()
+    copies[1].wait()
+    bottom = (held[:, :LAYER] * scale).astype(bf16)
+    top = (held[:, SLAB - LAYER :] * scale).astype(bf16)
+    even = near_layer > 0
+    near[:STEPS] = jnp.where(even, top, bottom)
+    far[:STEPS] = jnp.where(even, bottom, top)
+    copies[3].wait()
     picked = select_all(local, blocks, perm)
     for a in range(BS // STEPS):
         cut = slice(a * 2 * COL, (a + 1) * 2 * COL)
         near[STEPS:, cut] = picked[a * STEPS : (a + 1) * STEPS, : 2 * COL]
         far[STEPS:, cut] = picked[a * STEPS : (a + 1) * STEPS, 2 * COL :]
+    copies[2].wait()
 
 
 def edges(forcing, jac):
@@ -248,19 +240,18 @@
     return pl.pallas_call(
         edge_kernel,
         in_specs=[hbm, hbm],
-        out_shape=(edge, edge),
+        out_shape=(edge, edge, jax.ShapeDtypeStruct((STEPS, SLAB), f32)),
         scratch_shapes=[
-            pltpu.VMEM((2, STEPS, LAYER), f32),
             pltpu.VMEM((BS, BS, BLOCKS), bf16),
-            pltpu.SemaphoreType.DMA((3,)),
+            pltpu.SemaphoreType.DMA((4,)),
         ],
         name="edges",
-        compiler_params=pltpu.CompilerParams(vmem_limit_bytes=63 * 10**6),
+        compiler_params=pltpu.CompilerParams(vmem_limit_bytes=6 * 2**20),
         cost_estimate=cost(10**8, 2 * 10**6),
     )(forcing, jac)
 
 
-def jac_kernel(jac, near, far, box, local, sem):
+def jac_kernel(jac, far, near, box, local, sem):
     copy = pltpu.make_async_copy(jac, local, sem)
     copy.start()
     zg, yg, xg = box_of(lax.axis_index("tm"))
@@ -296,7 +287,7 @@
             box[:, 2 * p * COL : 2 * (p + 1) * COL] = value
 
 
-def select_jac(jac, near, far):
+def select_jac(jac, far, near):
     vmem = pl.BlockSpec(memory_space=pltpu.VMEM)
     return pl.pallas_call(
         jac_kernel,
@@ -306,7 +297,7 @@
         name="select_jac",
         compiler_params=pltpu.CompilerParams(vmem_limit_bytes=8 * 2**20),
         cost_estimate=cost(10**9, 2 * 10**6),
-    )(jac, near, far)
+    )(jac, far, near)
 
 
 def ops_kernel(main, mass, out, chosen, picked):
@@ -494,17 +485,18 @@
     across += [(j, i) for i, j in across]
     within += [(j, i) for i, j in within]
     jac = jnp.transpose(jacobi_inv, (1, 2, 0))
-    near, far = edges(forcing, jac)
+    forcing = pltpu.with_memory_space_constraint(forcing, pltpu.HBM)
+    far, near, held = edges(forcing, pltpu.with_memory_space_constraint(jac, pltpu.HBM))
     far = lax.ppermute(far, "space", across)
     near = lax.ppermute(near, "space", within)
-    packed = pack(forcing)
-    near, far, packed = lax.optimization_barrier((near, far, packed))
-    packed = patch(packed, near, far)
+    packed = pack(pltpu.with_memory_space_constraint(held, pltpu.VMEM))
+    far, near, packed = lax.optimization_barrier((far, near, packed))
+    packed = patch(packed, far, near)
     packed, op_main, op_mass = lax.optimization_barrier((packed, op_main, op_mass))
     recv = lax.all_to_all(packed, "tm", 0, 0).reshape(LENGTH, BOX)
     ops = select_ops(jnp.transpose(op_main, (1, 2, 0)), jnp.transpose(op_mass, (1, 2, 0)))
     ops, jac = lax.optimization_barrier((ops, jac))
-    box = select_jac(jac, near, far)
+    box = select_jac(jac, far, near)
     sent = solve(recv, ops, box)
     back = lax.all_to_all(sent, "tm", 0, 0)
     return unpack(back)

time: 52.6 us -> 51.5 us (0.979); the launches traced: 52.3 us -> 50.6 us
  starting transfers between devices: 9.16 us -> 11.1 us
  waiting for transfers between devices: 6.42 us -> 5.26 us
  Pallas kernels: 18 us -> 16.9 us
  local copies, waits for them, and re-layouts: 1.05 us -> 0.01 us
    ppermute x1, starting transfers between devices: 0.08 us -> 2.1 us  [per_device(): near = lax.ppermute(near, 'space', within)]
    unnamed x6 -> x4, local copies, waits for them, and re-layouts: 1.05 us -> 0.01 us
    pallas_call x2, Pallas kernels: 3.94 us -> 2.93 us  [the longest x1 1.89 us: edges(): pl.pallas_call(edge_kernel, in_specs=[hbm, hbm], out_shape=(edge, edge, j...]
    ppermute x1, waiting for transfers between devices: 1.31 us -> 0.52 us  [per_device(): far = lax.ppermute(far, 'space', across)]
where the time goes in v3:
time: 51.5 us; the launch traced here: 50.6 us
  Pallas kernels  16.9 us (33%)
  blocking collectives  16.6 us (32%)
  starting transfers between devices  11.1 us (22%)
  waiting for transfers between devices  5.26 us (10%)
  between operations  0.71 us (1%)
    all_to_all x1, blocking collectives, per_device(): back = lax.all_to_all(sent, 'tm', 0, 0)  16.6 us
    pallas_call x1, Pallas kernels, select_ops(): pl.pallas_call(ops_kernel, grid=(BS // CHUNK,), in_specs=[spec, spec], ou...  8.66 us
    all_to_all x1, starting transfers between devices, per_device(): recv = lax.all_to_all(packed, 'tm', 0, 0).reshape(LENGTH, BOX)  7.05 us
    all_to_all x1, waiting for transfers between devices, per_device(): recv = lax.all_to_all(packed, 'tm', 0, 0).reshape(LENGTH, BOX)  4.74 us
    ppermute x1, starting transfers between devices, per_device(): near = lax.ppermute(near, 'space', within)  2.1 us
    ppermute x1, starting transfers between devices, per_device(): far = lax.ppermute(far, 'space', across)  1.92 us
    pallas_call x1, Pallas kernels, edges(): pl.pallas_call(edge_kernel, in_specs=[hbm, hbm], out_shape=(edge, edge, j...  1.89 us
    pallas_call x1, Pallas kernels, solve(): pl.pallas_call(solve_kernel, out_shape=jax.ShapeDtypeStruct((PARTS, 3 * S...  1.68 us
  transfers between devices with their start and end apart: 3, of which 2 were waited for; matrix products, arithmetic and copies ran while one was open for 0% of the time, Pallas kernels for 22%

profile of v3, /device:TPU:32, one launch (start us, length us, event | category | flops | bytes accessed | tf_op | source)
XLA Modules:
  0.0 50.6 jit_solution(17526086914131604440)
XLA Ops:
  0.6 1.9 %edges.1 = (bf16[32,1024]{1,0:T(8,128)(2,1)S(1)}, bf16[32,1024]{1,0:T(8,128)(2,1)S(1)}, f32[16,8192]{1,0:T(8,128)S(1)}) custom-call(f32[16,8192]{1,0:T(8,128)} %forcing.1, bf16[64,64,128]{2,1,0:T(8,128)(2,1)} %bitcast.4), custom_call_target="tpu_custom_call" | custom-call | flops 100000000 | bytes 2000000 | tf_op jit(solution)/shard_map/edges/pallas_call | solution.py:240
  2.5 1.9 %collective-permute-start = (bf16[32,1024]{1,0:T(8,128)(2,1)S(1)}, bf16[32,1024]{1,0:T(8,128)(2,1)S(1)}, u32[]{:S(2)}, u32[]{:S(2)}) collective-permute-start(bf16[32,1024]{1,0:T(8,128)(2,1)S(1)} %get-tuple-element.14), channel_id=1, source_target_pairs={{1,2},{3,4},{5,6},{2,1},{4,3},{6,5},{9,10},{11,12},{13,14},{10,9},... | collective-permute-start | bytes 196616 | tf_op jit(solution)/shard_map/ppermute | solution.py:490
  4.5 2.1 %collective-permute-start.1 = (bf16[32,1024]{1,0:T(8,128)(2,1)S(1)}, bf16[32,1024]{1,0:T(8,128)(2,1)S(1)}, u32[]{:S(2)}, u32[]{:S(2)}) collective-permute-start(bf16[32,1024]{1,0:T(8,128)(2,1)S(1)} %get-tuple-element.15), channel_id=1, source_target_pairs={{0,1},{2,3},{4,5},{6,7},{1,0},{3,2},{5,4},{7,6},{8,9},{10,11},{12,... | collective-permute-start | bytes 196616 | tf_op jit(solution)/shard_map/ppermute | solution.py:491
  6.6 1.0 %pack.1.packed = bf16[16,16,1536]{2,1,0:T(8,128)(2,1)} custom-call(f32[16,8192]{1,0:T(8,128)S(1)} %get-tuple-element.16.forcing), custom_call_target="tpu_custom_call" | custom-call | flops 1000000 | bytes 4000000 | tf_op jit(solution)/shard_map/pack/pallas_call | solution.py:102
  7.6 0.5 %collective-permute-done.far = bf16[32,1024]{1,0:T(8,128)(2,1)S(1)} collective-permute-done((bf16[32,1024]{1,0:T(8,128)(2,1)S(1)}, bf16[32,1024]{1,0:T(8,128)(2,1)S(1)}, u32[]{:S(2)}, u32[]{:S(2)}) %collective-permute-start) | collective-permute-done | bytes 65568 | tf_op jit(solution)/shard_map/ppermute | solution.py:490
  8.1 0.0 collective-permute-done.1.near
  8.1 0.8 %patch.1 = bf16[16,16,1536]{2,1,0:T(8,128)(2,1)} custom-call(bf16[16,16,1536]{2,1,0:T(8,128)(2,1)} %pack.1.packed, bf16[32,1024]{1,0:T(8,128)(2,1)S(1)} %collective-permute-done.far, bf16[32,1024]{1,0:T(8,128)(2,1)S(1)} %collective-permute-done.1.near), custom_call_target="tpu_custom_call", output_to_operand_aliasing={{}: (0, {})} | custom-call | flops 1000 | bytes 200000 | tf_op jit(solution)/shard_map/patch/pallas_call | solution.py:146
  8.9 7.0 %all-to-all-start = ((bf16[16,16,1536]{2,1,0:T(8,128)(2,1)}), bf16[16,16,1536]{2,1,0:T(8,128)(2,1)S(1)}, u32[]{:S(2)}, u32[]{:S(2)}) async-start(bf16[16,16,1536]{2,1,0:T(8,128)(2,1)} %patch.1), calls=%async_computation | async-start | bytes 1572864 | tf_op jit(solution)/shard_map/all_to_all | solution.py:496
  16.0 0.0 copy-start
  16.0 0.0 copy-start.1
  16.0 8.7 %select_ops.1.ops = bf16[4,768,256]{2,1,0:T(8,128)(2,1)S(1)} custom-call(bf16[64,448,128]{2,1,0:T(8,128)(2,1)} %bitcast.7, bf16[64,448,128]{2,1,0:T(8,128)(2,1)} %bitcast.8), custom_call_target="tpu_custom_call" | custom-call | flops 4000000000 | bytes 16000000 | tf_op jit(solution)/shard_map/select_ops/pallas_call | solution.py:361
  24.7 0.0 copy-done
  24.7 1.6 %select_jac.1.box = bf16[64,1536]{1,0:T(8,128)(2,1)S(1)} custom-call(bf16[64,64,128]{2,1,0:T(8,128)(2,1)S(1)} %bitcast.5, bf16[32,1024]{1,0:T(8,128)(2,1)S(1)} %collective-permute-done.far, bf16[32,1024]{1,0:T(8,128)(2,1)S(1)} %collective-permute-done.1.near), custom_call_target="tpu_custom_call" | custom-call | flops 1000000000 | bytes 2000000 | tf_op jit(solution)/shard_map/select_jac/pallas_call | solution.py:292
  26.3 4.7 %all-to-all-done = bf16[16,16,1536]{2,1,0:T(8,128)(2,1)S(1)} async-done(((bf16[16,16,1536]{2,1,0:T(8,128)(2,1)}), bf16[16,16,1536]{2,1,0:T(8,128)(2,1)S(1)}, u32[]{:S(2)}, u32[]{:S(2)}) %all-to-all-start) | async-done | bytes 786464 | tf_op jit(solution)/shard_map/all_to_all | solution.py:496
  31.1 0.0 copy-done.1
  31.1 1.7 %solve.1 = bf16[16,48,512]{2,1,0:T(8,128)(2,1)S(1)} custom-call(bf16[256,1536]{1,0:T(8,128)(2,1)S(1)} %bitcast.6, bf16[4,768,256]{2,1,0:T(8,128)(2,1)S(1)} %select_ops.1.ops, bf16[64,1536]{1,0:T(8,128)(2,1)S(1)} %select_jac.1.box, bf16[512,768]{1,0:T(8,128)(2,1)S(1)} %copy-done.1), custom_call_target="tpu_custom_call" | custom-call | flops 3000000000 | bytes 5000000 | tf_op jit(solution)/shard_map/solve/pallas_call | solution.py:433
  32.7 16.6 %all_to_all.10.recv = bf16[16,48,512]{2,1,0:T(8,128)(2,1)S(1)} all-to-all(bf16[16,48,512]{2,1,0:T(8,128)(2,1)S(1)} %solve.1), channel_id=1, replica_groups=mesh['tm'=16,'space'=8] {'tm'}, dimensions={0} | all-to-all | bytes 1572864 | tf_op jit(solution)/shard_map/all_to_all | solution.py:501
  49.3 1.2 %unpack.1 = (f32[16,8192]{1,0:T(8,128)}, f32[16,8192]{1,0:T(8,128)}, f32[16,8192]{1,0:T(8,128)}) custom-call(bf16[16,48,512]{2,1,0:T(8,128)(2,1)S(1)} %all_to_all.10.recv), custom_call_target="tpu_custom_call" | custom-call | flops 1000000 | bytes 3000000 | tf_op jit(solution)/shard_map/unpack/pallas_call | solution.py:470
Async XLA Ops:
  2.5 5.6 %collective-permute-start = (bf16[32,1024]{1,0:T(8,128)(2,1)S(1)}, bf16[32,1024]{1,0:T(8,128)(2,1)S(1)}, u32[]{:S(2)}, u32[]{:S(2)}) collective-permute-start(bf16[32,1024]{1,0:T(8,128)(2,1)S(1)} %get-tuple-element.14), channel_id=1, source_target_pairs={{1,2},{3,4},{5,6},{2,1},{4,3},{6,5},{9,10},{11,12},{13,14},{10,9},... | collective-permute-start | bytes 196616 | tf_op jit(solution)/shard_map/ppermute | solution.py:490
  4.5 3.7 %collective-permute-start.1 = (bf16[32,1024]{1,0:T(8,128)(2,1)S(1)}, bf16[32,1024]{1,0:T(8,128)(2,1)S(1)}, u32[]{:S(2)}, u32[]{:S(2)}) collective-permute-start(bf16[32,1024]{1,0:T(8,128)(2,1)S(1)} %get-tuple-element.15), channel_id=1, source_target_pairs={{0,1},{2,3},{4,5},{6,7},{1,0},{3,2},{5,4},{7,6},{8,9},{10,11},{12,... | collective-permute-start | bytes 196616 | tf_op jit(solution)/shard_map/ppermute | solution.py:491
  8.9 22.1 %all-to-all-start = ((bf16[16,16,1536]{2,1,0:T(8,128)(2,1)}), bf16[16,16,1536]{2,1,0:T(8,128)(2,1)S(1)}, u32[]{:S(2)}, u32[]{:S(2)}) async-start(bf16[16,16,1536]{2,1,0:T(8,128)(2,1)} %patch.1), calls=%async_computation | async-start | bytes 1572864 | tf_op jit(solution)/shard_map/all_to_all | solution.py:496
  16.0 8.7 %copy-start = (bf16[128,64,64]{0,2,1:T(8,128)(2,1)S(1)}, bf16[128,64,64]{0,2,1:T(8,128)(2,1)}, u32[]{:S(2)}) copy-start(bf16[128,64,64]{0,2,1:T(8,128)(2,1)} %param.8) | copy-start | bytes 3145732
  16.0 15.1 %copy-start.1 = (bf16[512,768]{1,0:T(8,128)(2,1)S(1)}, bf16[512,768]{1,0:T(8,128)(2,1)}, u32[]{:S(2)}) copy-start(bf16[512,768]{1,0:T(8,128)(2,1)} %constant.2.clone.table) | copy-start | bytes 2359300

commit v4 on v3

--- a/solution.py
+++ b/solution.py
@@ -116,15 +116,14 @@
             zg, yg, xg = box_of(dest)
             for edge, at_group, first in ((low_edge, 0, 4), (high_edge, 3, 6)):
                 if zg == at_group:
-                    for d in range(2):
-                        at = (2 * yg + d) * ROW + xg * COL
-                        copies.append(
-                            pltpu.make_async_copy(
-                                edge.at[pl.ds(0, STEPS), pl.ds(at, COL)],
-                                out.at[dest, :, pl.ds((first + d) * COL, COL)],
-                                sems.at[len(copies)],
-                            )
+                    at = (2 * yg + xg) * 2 * COL
+                    copies.append(
+                        pltpu.make_async_copy(
+                            edge.at[pl.ds(0, STEPS), pl.ds(at, 2 * COL)],
+                            out.at[dest, :, pl.ds(first * COL, 2 * COL)],
+                            sems.at[len(copies)],
                         )
+                    )
         for copy in copies:
             copy.start()
         for copy in copies:
@@ -148,7 +147,7 @@
         in_specs=[anywhere] * 3,
         out_specs=anywhere,
         out_shape=jax.ShapeDtypeStruct((PARTS, STEPS, BOX), bf16),
-        scratch_shapes=[pltpu.SemaphoreType.DMA((16,))],
+        scratch_shapes=[pltpu.SemaphoreType.DMA((8,))],
         input_output_aliases={0: 0},
         name="patch",
         compiler_params=pltpu.CompilerParams(vmem_limit_bytes=2**20),
@@ -179,7 +178,7 @@
     return dot(rows, chosen).astype(bf16)
 
 
-def select_all(jac, blocks, perm):
+def select_all(jac, chosen, perm):
     chunks = BS // CHUNK
     rows = jnp.concatenate(
         [
@@ -188,7 +187,7 @@
         ],
         axis=1,
     )
-    picked = dot(rows, selector(blocks, COL)).astype(bf16)
+    picked = dot(rows, chosen).astype(bf16)
     side = jnp.concatenate([picked[c * BS : (c + 1) * BS] for c in range(chunks)], axis=1)
     return dot(side, perm).astype(bf16)
 
@@ -210,23 +209,33 @@
         pltpu.make_async_copy(forcing.at[:, cut], held.at[:, cut], sems.at[which])
         for which, cut in enumerate(cuts)
     ]
-    copies.append(pltpu.make_async_copy(jac, local, sems.at[3]))
-    for which in (0, 1, 3, 2):
+    for c in range(BS // CHUNK):
+        cut = pl.ds(c * CHUNK, CHUNK)
+        copies.append(pltpu.make_async_copy(jac.at[cut], local.at[cut], sems.at[3 + c]))
+    for which in (0, 1, 3, 4, 5, 6, 2):
         copies[which].start()
-    scale = jnp.concatenate([scales()] * (LAYER // COL), axis=1)
+    scale = scales()
     slot = slots_of()
     layer = jnp.where(slot < 4, near_layer, LAYERS - 1 - near_layer)
-    blocks = block_at(layer, 2 * yg + slot // 2 % 2, 2 * xg + slot % 2)
+    chosen = selector(
+        block_at(layer, 2 * yg + slot // 2 % 2, 2 * xg + slot % 2), COL
+    )
     perm = reorder(4 * COL)
     copies[0].wait()
     copies[1].wait()
-    bottom = (held[:, :LAYER] * scale).astype(bf16)
-    top = (held[:, SLAB - LAYER :] * scale).astype(bf16)
     even = near_layer > 0
-    near[:STEPS] = jnp.where(even, top, bottom)
-    far[:STEPS] = jnp.where(even, bottom, top)
-    copies[3].wait()
-    picked = select_all(local, blocks, perm)
+    for target in range(4):
+        for d in range(2):
+            at = (2 * (target // 2) + d) * ROW + target % 2 * COL
+            to = slice((2 * target + d) * COL, (2 * target + d + 1) * COL)
+            bottom = (held[:, at : at + COL] * scale).astype(bf16)
+            at += SLAB - LAYER
+            top = (held[:, at : at + COL] * scale).astype(bf16)
+            near[:STEPS, to] = jnp.where(even, top, bottom)
+            far[:STEPS, to] = jnp.where(even, bottom, top)
+    for c in range(BS // CHUNK):
+        copies[3 + c].wait()
+    picked = select_all(local, chosen, perm)
     for a in range(BS // STEPS):
         cut = slice(a * 2 * COL, (a + 1) * 2 * COL)
         near[STEPS:, cut] = picked[a * STEPS : (a + 1) * STEPS, : 2 * COL]
@@ -243,7 +252,7 @@
         out_shape=(edge, edge, jax.ShapeDtypeStruct((STEPS, SLAB), f32)),
         scratch_shapes=[
             pltpu.VMEM((BS, BS, BLOCKS), bf16),
-            pltpu.SemaphoreType.DMA((4,)),
+            pltpu.SemaphoreType.DMA((7,)),
         ],
         name="edges",
         compiler_params=pltpu.CompilerParams(vmem_limit_bytes=6 * 2**20),
@@ -276,7 +285,7 @@
 
     near, far = other(near), other(far)
     for at, blocks in enumerate((own, faces, jnp.where(first, beside, ahead))):
-        both = select_all(local, blocks, perm)
+        both = select_all(local, selector(blocks, COL), perm)
         for which in range(2):
             value = both[:, which * 2 * COL : (which + 1) * 2 * COL]
             if at == 1 and which == 0:

time: 51.5 us -> 51.4 us (level)
  no operation moved by 1% of the time
where the time goes in v4:
time: 51.4 us; the launch traced here: 50.4 us
  Pallas kernels  16.8 us (33%)
  blocking collectives  16.6 us (32%)
  starting transfers between devices  11.1 us (22%)
  waiting for transfers between devices  5.26 us (10%)
  between operations  0.71 us (1%)
    all_to_all x1, blocking collectives, per_device(): back = lax.all_to_all(sent, 'tm', 0, 0)  16.6 us
    pallas_call x1, Pallas kernels, select_ops(): pl.pallas_call(ops_kernel, grid=(BS // CHUNK,), in_specs=[spec, spec], ou...  8.66 us
    all_to_all x1, starting transfers between devices, per_device(): recv = lax.all_to_all(packed, 'tm', 0, 0).reshape(LENGTH, BOX)  7.05 us
    all_to_all x1, waiting for transfers between devices, per_device(): recv = lax.all_to_all(packed, 'tm', 0, 0).reshape(LENGTH, BOX)  4.74 us
    ppermute x1, starting transfers between devices, per_device(): near = lax.ppermute(near, 'space', within)  2.11 us
    ppermute x1, starting transfers between devices, per_device(): far = lax.ppermute(far, 'space', across)  1.92 us
    pallas_call x1, Pallas kernels, edges(): pl.pallas_call(edge_kernel, in_specs=[hbm, hbm], out_shape=(edge, edge, j...  1.87 us
    pallas_call x1, Pallas kernels, solve(): pl.pallas_call(solve_kernel, out_shape=jax.ShapeDtypeStruct((PARTS, 3 * S...  1.68 us
  transfers between devices with their start and end apart: 3, of which 2 were waited for; matrix products, arithmetic and copies ran while one was open for 0% of the time, Pallas kernels for 22%

profile of v4, /device:TPU:32, one launch (start us, length us, event | category | flops | bytes accessed | tf_op | source)
XLA Modules:
  0.0 50.4 jit_solution(1303762899316098666)
XLA Ops:
  0.6 1.9 %edges.1 = (bf16[32,1024]{1,0:T(8,128)(2,1)S(1)}, bf16[32,1024]{1,0:T(8,128)(2,1)S(1)}, f32[16,8192]{1,0:T(8,128)S(1)}) custom-call(f32[16,8192]{1,0:T(8,128)} %forcing.1, bf16[64,64,128]{2,1,0:T(8,128)(2,1)} %bitcast.4), custom_call_target="tpu_custom_call" | custom-call | flops 100000000 | bytes 2000000 | tf_op jit(solution)/shard_map/edges/pallas_call | solution.py:249
  2.5 1.9 %collective-permute-start = (bf16[32,1024]{1,0:T(8,128)(2,1)S(1)}, bf16[32,1024]{1,0:T(8,128)(2,1)S(1)}, u32[]{:S(2)}, u32[]{:S(2)}) collective-permute-start(bf16[32,1024]{1,0:T(8,128)(2,1)S(1)} %get-tuple-element.14), channel_id=1, source_target_pairs={{1,2},{3,4},{5,6},{2,1},{4,3},{6,5},{9,10},{11,12},{13,14},{10,9},... | collective-permute-start | bytes 196616 | tf_op jit(solution)/shard_map/ppermute | solution.py:499
  4.4 2.1 %collective-permute-start.1 = (bf16[32,1024]{1,0:T(8,128)(2,1)S(1)}, bf16[32,1024]{1,0:T(8,128)(2,1)S(1)}, u32[]{:S(2)}, u32[]{:S(2)}) collective-permute-start(bf16[32,1024]{1,0:T(8,128)(2,1)S(1)} %get-tuple-element.15), channel_id=1, source_target_pairs={{0,1},{2,3},{4,5},{6,7},{1,0},{3,2},{5,4},{7,6},{8,9},{10,11},{12,... | collective-permute-start | bytes 196616 | tf_op jit(solution)/shard_map/ppermute | solution.py:500
  6.5 1.0 %pack.1.packed = bf16[16,16,1536]{2,1,0:T(8,128)(2,1)} custom-call(f32[16,8192]{1,0:T(8,128)S(1)} %get-tuple-element.16.forcing), custom_call_target="tpu_custom_call" | custom-call | flops 1000000 | bytes 4000000 | tf_op jit(solution)/shard_map/pack/pallas_call | solution.py:102
  7.6 0.5 %collective-permute-done.far = bf16[32,1024]{1,0:T(8,128)(2,1)S(1)} collective-permute-done((bf16[32,1024]{1,0:T(8,128)(2,1)S(1)}, bf16[32,1024]{1,0:T(8,128)(2,1)S(1)}, u32[]{:S(2)}, u32[]{:S(2)}) %collective-permute-start) | collective-permute-done | bytes 65568 | tf_op jit(solution)/shard_map/ppermute | solution.py:499
  8.1 0.0 collective-permute-done.1.near
  8.1 0.7 %patch.1 = bf16[16,16,1536]{2,1,0:T(8,128)(2,1)} custom-call(bf16[16,16,1536]{2,1,0:T(8,128)(2,1)} %pack.1.packed, bf16[32,1024]{1,0:T(8,128)(2,1)S(1)} %collective-permute-done.far, bf16[32,1024]{1,0:T(8,128)(2,1)S(1)} %collective-permute-done.1.near), custom_call_target="tpu_custom_call", output_to_operand_aliasing={{}: (0, {})} | custom-call | flops 1000 | bytes 200000 | tf_op jit(solution)/shard_map/patch/pallas_call | solution.py:145
  8.8 7.1 %all-to-all-start = ((bf16[16,16,1536]{2,1,0:T(8,128)(2,1)}), bf16[16,16,1536]{2,1,0:T(8,128)(2,1)S(1)}, u32[]{:S(2)}, u32[]{:S(2)}) async-start(bf16[16,16,1536]{2,1,0:T(8,128)(2,1)} %patch.1), calls=%async_computation | async-start | bytes 1572864 | tf_op jit(solution)/shard_map/all_to_all | solution.py:505
  15.9 0.0 copy-start
  15.9 0.0 copy-start.1
  15.9 8.7 %select_ops.1.ops = bf16[4,768,256]{2,1,0:T(8,128)(2,1)S(1)} custom-call(bf16[64,448,128]{2,1,0:T(8,128)(2,1)} %bitcast.7, bf16[64,448,128]{2,1,0:T(8,128)(2,1)} %bitcast.8), custom_call_target="tpu_custom_call" | custom-call | flops 4000000000 | bytes 16000000 | tf_op jit(solution)/shard_map/select_ops/pallas_call | solution.py:370
  24.6 0.0 copy-done
  24.6 1.6 %select_jac.1.box = bf16[64,1536]{1,0:T(8,128)(2,1)S(1)} custom-call(bf16[64,64,128]{2,1,0:T(8,128)(2,1)S(1)} %bitcast.5, bf16[32,1024]{1,0:T(8,128)(2,1)S(1)} %collective-permute-done.far, bf16[32,1024]{1,0:T(8,128)(2,1)S(1)} %collective-permute-done.1.near), custom_call_target="tpu_custom_call" | custom-call | flops 1000000000 | bytes 2000000 | tf_op jit(solution)/shard_map/select_jac/pallas_call | solution.py:301
  26.2 4.7 %all-to-all-done = bf16[16,16,1536]{2,1,0:T(8,128)(2,1)S(1)} async-done(((bf16[16,16,1536]{2,1,0:T(8,128)(2,1)}), bf16[16,16,1536]{2,1,0:T(8,128)(2,1)S(1)}, u32[]{:S(2)}, u32[]{:S(2)}) %all-to-all-start) | async-done | bytes 786464 | tf_op jit(solution)/shard_map/all_to_all | solution.py:505
  31.0 0.0 copy-done.1
  31.0 1.7 %solve.1 = bf16[16,48,512]{2,1,0:T(8,128)(2,1)S(1)} custom-call(bf16[256,1536]{1,0:T(8,128)(2,1)S(1)} %bitcast.6, bf16[4,768,256]{2,1,0:T(8,128)(2,1)S(1)} %select_ops.1.ops, bf16[64,1536]{1,0:T(8,128)(2,1)S(1)} %select_jac.1.box, bf16[512,768]{1,0:T(8,128)(2,1)S(1)} %copy-done.1), custom_call_target="tpu_custom_call" | custom-call | flops 3000000000 | bytes 5000000 | tf_op jit(solution)/shard_map/solve/pallas_call | solution.py:442
  32.6 16.6 %all_to_all.10.recv = bf16[16,48,512]{2,1,0:T(8,128)(2,1)S(1)} all-to-all(bf16[16,48,512]{2,1,0:T(8,128)(2,1)S(1)} %solve.1), channel_id=1, replica_groups=mesh['tm'=16,'space'=8] {'tm'}, dimensions={0} | all-to-all | bytes 1572864 | tf_op jit(solution)/shard_map/all_to_all | solution.py:510
  49.2 1.2 %unpack.1 = (f32[16,8192]{1,0:T(8,128)}, f32[16,8192]{1,0:T(8,128)}, f32[16,8192]{1,0:T(8,128)}) custom-call(bf16[16,48,512]{2,1,0:T(8,128)(2,1)S(1)} %all_to_all.10.recv), custom_call_target="tpu_custom_call" | custom-call | flops 1000000 | bytes 3000000 | tf_op jit(solution)/shard_map/unpack/pallas_call | solution.py:479
Async XLA Ops:
  2.5 5.6 %collective-permute-start = (bf16[32,1024]{1,0:T(8,128)(2,1)S(1)}, bf16[32,1024]{1,0:T(8,128)(2,1)S(1)}, u32[]{:S(2)}, u32[]{:S(2)}) collective-permute-start(bf16[32,1024]{1,0:T(8,128)(2,1)S(1)} %get-tuple-element.14), channel_id=1, source_target_pairs={{1,2},{3,4},{5,6},{2,1},{4,3},{6,5},{9,10},{11,12},{13,14},{10,9},... | collective-permute-start | bytes 196616 | tf_op jit(solution)/shard_map/ppermute | solution.py:499
  4.4 3.7 %collective-permute-start.1 = (bf16[32,1024]{1,0:T(8,128)(2,1)S(1)}, bf16[32,1024]{1,0:T(8,128)(2,1)S(1)}, u32[]{:S(2)}, u32[]{:S(2)}) collective-permute-start(bf16[32,1024]{1,0:T(8,128)(2,1)S(1)} %get-tuple-element.15), channel_id=1, source_target_pairs={{0,1},{2,3},{4,5},{6,7},{1,0},{3,2},{5,4},{7,6},{8,9},{10,11},{12,... | collective-permute-start | bytes 196616 | tf_op jit(solution)/shard_map/ppermute | solution.py:500
  8.8 22.1 %all-to-all-start = ((bf16[16,16,1536]{2,1,0:T(8,128)(2,1)}), bf16[16,16,1536]{2,1,0:T(8,128)(2,1)S(1)}, u32[]{:S(2)}, u32[]{:S(2)}) async-start(bf16[16,16,1536]{2,1,0:T(8,128)(2,1)} %patch.1), calls=%async_computation | async-start | bytes 1572864 | tf_op jit(solution)/shard_map/all_to_all | solution.py:505
  15.9 8.7 %copy-start = (bf16[128,64,64]{0,2,1:T(8,128)(2,1)S(1)}, bf16[128,64,64]{0,2,1:T(8,128)(2,1)}, u32[]{:S(2)}) copy-start(bf16[128,64,64]{0,2,1:T(8,128)(2,1)} %param.8) | copy-start | bytes 3145732
  15.9 15.1 %copy-start.1 = (bf16[512,768]{1,0:T(8,128)(2,1)S(1)}, bf16[512,768]{1,0:T(8,128)(2,1)}, u32[]{:S(2)}) copy-start(bf16[512,768]{1,0:T(8,128)(2,1)} %constant.2.clone.table) | copy-start | bytes 2359300

commit v5 on v4

--- a/solution.py
+++ b/solution.py
@@ -111,19 +111,16 @@
 
 def patch_kernel(packed, far, near, out, sems):
     def place(low_edge, high_edge):
-        copies = []
-        for dest in range(PARTS):
-            zg, yg, xg = box_of(dest)
-            for edge, at_group, first in ((low_edge, 0, 4), (high_edge, 3, 6)):
-                if zg == at_group:
-                    at = (2 * yg + xg) * 2 * COL
-                    copies.append(
-                        pltpu.make_async_copy(
-                            edge.at[pl.ds(0, STEPS), pl.ds(at, 2 * COL)],
-                            out.at[dest, :, pl.ds(first * COL, 2 * COL)],
-                            sems.at[len(copies)],
-                        )
-                    )
+        copies = [
+            pltpu.make_async_copy(
+                edge.at[pl.ds(0, 4)],
+                out.at[pl.ds(first_dest, 4), :, pl.ds(first * COL, 2 * COL)],
+                sems.at[which],
+            )
+            for which, (edge, first_dest, first) in enumerate(
+                ((low_edge, 0, 4), (high_edge, PARTS - 4, 6))
+            )
+        ]
         for copy in copies:
             copy.start()
         for copy in copies:
@@ -147,7 +144,7 @@
         in_specs=[anywhere] * 3,
         out_specs=anywhere,
         out_shape=jax.ShapeDtypeStruct((PARTS, STEPS, BOX), bf16),
-        scratch_shapes=[pltpu.SemaphoreType.DMA((8,))],
+        scratch_shapes=[pltpu.SemaphoreType.DMA((2,))],
         input_output_aliases={0: 0},
         name="patch",
         compiler_params=pltpu.CompilerParams(vmem_limit_bytes=2**20),
@@ -227,24 +224,24 @@
     for target in range(4):
         for d in range(2):
             at = (2 * (target // 2) + d) * ROW + target % 2 * COL
-            to = slice((2 * target + d) * COL, (2 * target + d + 1) * COL)
+            to = slice(d * COL, (d + 1) * COL)
             bottom = (held[:, at : at + COL] * scale).astype(bf16)
             at += SLAB - LAYER
             top = (held[:, at : at + COL] * scale).astype(bf16)
-            near[:STEPS, to] = jnp.where(even, top, bottom)
-            far[:STEPS, to] = jnp.where(even, bottom, top)
+            near[target, :, to] = jnp.where(even, top, bottom)
+            far[target, :, to] = jnp.where(even, bottom, top)
     for c in range(BS // CHUNK):
         copies[3 + c].wait()
     picked = select_all(local, chosen, perm)
     for a in range(BS // STEPS):
-        cut = slice(a * 2 * COL, (a + 1) * 2 * COL)
-        near[STEPS:, cut] = picked[a * STEPS : (a + 1) * STEPS, : 2 * COL]
-        far[STEPS:, cut] = picked[a * STEPS : (a + 1) * STEPS, 2 * COL :]
+        rows = slice(a * STEPS, (a + 1) * STEPS)
+        near[4 + a] = picked[rows, : 2 * COL]
+        far[4 + a] = picked[rows, 2 * COL :]
     copies[2].wait()
 
 
 def edges(forcing, jac):
-    edge = jax.ShapeDtypeStruct((2 * STEPS, LAYER), bf16)
+    edge = jax.ShapeDtypeStruct((4 + BS // STEPS, STEPS, 2 * COL), bf16)
     hbm = pl.BlockSpec(memory_space=pltpu.HBM)
     return pl.pallas_call(
         edge_kernel,
@@ -280,8 +277,7 @@
     even = lax.axis_index("space") % 2 == 0
 
     def other(edge):
-        pieces = [edge[STEPS:, 2 * a * COL : 2 * (a + 1) * COL] for a in range(BS // STEPS)]
-        return jnp.concatenate(pieces, axis=0)
+        return jnp.concatenate([edge[4 + a] for a in range(BS // STEPS)], axis=0)
 
     near, far = other(near), other(far)
     for at, blocks in enumerate((own, faces, jnp.where(first, beside, ahead))):

time: 51.4 us -> 51.3 us (level)
  no operation moved by 1% of the time
where the time goes in v5:
time: 51.3 us; the launch traced here: 50.4 us
  Pallas kernels  16.8 us (33%)
  blocking collectives  16.6 us (32%)
  starting transfers between devices  11.1 us (22%)
  waiting for transfers between devices  5.26 us (10%)
  between operations  0.71 us (1%)
    all_to_all x1, blocking collectives, per_device(): back = lax.all_to_all(sent, 'tm', 0, 0)  16.6 us
    pallas_call x1, Pallas kernels, select_ops(): pl.pallas_call(ops_kernel, grid=(BS // CHUNK,), in_specs=[spec, spec], ou...  8.66 us
    all_to_all x1, starting transfers between devices, per_device(): recv = lax.all_to_all(packed, 'tm', 0, 0).reshape(LENGTH, BOX)  7.05 us
    all_to_all x1, waiting for transfers between devices, per_device(): recv = lax.all_to_all(packed, 'tm', 0, 0).reshape(LENGTH, BOX)  4.74 us
    ppermute x1, starting transfers between devices, per_device(): near = lax.ppermute(near, 'space', within)  2.11 us
    ppermute x1, starting transfers between devices, per_device(): far = lax.ppermute(far, 'space', across)  1.92 us
    pallas_call x1, Pallas kernels, edges(): pl.pallas_call(edge_kernel, in_specs=[hbm, hbm], out_shape=(edge, edge, j...  1.87 us
    pallas_call x1, Pallas kernels, solve(): pl.pallas_call(solve_kernel, out_shape=jax.ShapeDtypeStruct((PARTS, 3 * S...  1.68 us
  transfers between devices with their start and end apart: 3, of which 2 were waited for; matrix products, arithmetic and copies ran while one was open for 0% of the time, Pallas kernels for 22%

profile of v5, /device:TPU:32, one launch (start us, length us, event | category | flops | bytes accessed | tf_op | source)
XLA Modules:
  0.0 50.4 jit_solution(12469685311726147530)
XLA Ops:
  0.6 1.9 %edges.1 = (bf16[8,16,256]{2,1,0:T(8,128)(2,1)S(1)}, bf16[8,16,256]{2,1,0:T(8,128)(2,1)S(1)}, f32[16,8192]{1,0:T(8,128)S(1)}) custom-call(f32[16,8192]{1,0:T(8,128)} %forcing.1, bf16[64,64,128]{2,1,0:T(8,128)(2,1)} %bitcast.4), custom_call_target="tpu_custom_call" | custom-call | flops 100000000 | bytes 2000000 | tf_op jit(solution)/shard_map/edges/pallas_call | solution.py:246
  2.5 1.9 %collective-permute-start = (bf16[8,16,256]{2,1,0:T(8,128)(2,1)S(1)}, bf16[8,16,256]{2,1,0:T(8,128)(2,1)S(1)}, u32[]{:S(2)}, u32[]{:S(2)}) collective-permute-start(bf16[8,16,256]{2,1,0:T(8,128)(2,1)S(1)} %get-tuple-element.14), channel_id=1, source_target_pairs={{1,2},{3,4},{5,6},{2,1},{4,3},{6,5},{9,10},{11,12},{13,14},{10,9},... | collective-permute-start | bytes 196616 | tf_op jit(solution)/shard_map/ppermute | solution.py:495
  4.4 2.1 %collective-permute-start.1 = (bf16[8,16,256]{2,1,0:T(8,128)(2,1)S(1)}, bf16[8,16,256]{2,1,0:T(8,128)(2,1)S(1)}, u32[]{:S(2)}, u32[]{:S(2)}) collective-permute-start(bf16[8,16,256]{2,1,0:T(8,128)(2,1)S(1)} %get-tuple-element.15), channel_id=1, source_target_pairs={{0,1},{2,3},{4,5},{6,7},{1,0},{3,2},{5,4},{7,6},{8,9},{10,11},{12,... | collective-permute-start | bytes 196616 | tf_op jit(solution)/shard_map/ppermute | solution.py:496
  6.5 1.0 %pack.1.packed = bf16[16,16,1536]{2,1,0:T(8,128)(2,1)} custom-call(f32[16,8192]{1,0:T(8,128)S(1)} %get-tuple-element.16.forcing), custom_call_target="tpu_custom_call" | custom-call | flops 1000000 | bytes 4000000 | tf_op jit(solution)/shard_map/pack/pallas_call | solution.py:102
  7.6 0.5 %collective-permute-done.far = bf16[8,16,256]{2,1,0:T(8,128)(2,1)S(1)} collective-permute-done((bf16[8,16,256]{2,1,0:T(8,128)(2,1)S(1)}, bf16[8,16,256]{2,1,0:T(8,128)(2,1)S(1)}, u32[]{:S(2)}, u32[]{:S(2)}) %collective-permute-start) | collective-permute-done | bytes 65568 | tf_op jit(solution)/shard_map/ppermute | solution.py:495
  8.1 0.0 collective-permute-done.1.near
  8.1 0.6 %patch.1 = bf16[16,16,1536]{2,1,0:T(8,128)(2,1)} custom-call(bf16[16,16,1536]{2,1,0:T(8,128)(2,1)} %pack.1.packed, bf16[8,16,256]{2,1,0:T(8,128)(2,1)S(1)} %collective-permute-done.far, bf16[8,16,256]{2,1,0:T(8,128)(2,1)S(1)} %collective-permute-done.1.near), custom_call_target="tpu_custom_call", output_to_operand_aliasing={{}: (0, {})} | custom-call | flops 1000 | bytes 200000 | tf_op jit(solution)/shard_map/patch/pallas_call | solution.py:142
  8.7 7.1 %all-to-all-start = ((bf16[16,16,1536]{2,1,0:T(8,128)(2,1)}), bf16[16,16,1536]{2,1,0:T(8,128)(2,1)S(1)}, u32[]{:S(2)}, u32[]{:S(2)}) async-start(bf16[16,16,1536]{2,1,0:T(8,128)(2,1)} %patch.1), calls=%async_computation | async-start | bytes 1572864 | tf_op jit(solution)/shard_map/all_to_all | solution.py:501
  15.8 0.0 copy-start
  15.8 0.0 copy-start.1
  15.8 8.7 %select_ops.1.ops = bf16[4,768,256]{2,1,0:T(8,128)(2,1)S(1)} custom-call(bf16[64,448,128]{2,1,0:T(8,128)(2,1)} %bitcast.7, bf16[64,448,128]{2,1,0:T(8,128)(2,1)} %bitcast.8), custom_call_target="tpu_custom_call" | custom-call | flops 4000000000 | bytes 16000000 | tf_op jit(solution)/shard_map/select_ops/pallas_call | solution.py:366
  24.5 0.0 copy-done
  24.5 1.6 %select_jac.1.box = bf16[64,1536]{1,0:T(8,128)(2,1)S(1)} custom-call(bf16[64,64,128]{2,1,0:T(8,128)(2,1)S(1)} %bitcast.5, bf16[8,16,256]{2,1,0:T(8,128)(2,1)S(1)} %collective-permute-done.far, bf16[8,16,256]{2,1,0:T(8,128)(2,1)S(1)} %collective-permute-done.1.near), custom_call_target="tpu_custom_call" | custom-call | flops 1000000000 | bytes 2000000 | tf_op jit(solution)/shard_map/select_jac/pallas_call | solution.py:297
  26.1 4.7 %all-to-all-done = bf16[16,16,1536]{2,1,0:T(8,128)(2,1)S(1)} async-done(((bf16[16,16,1536]{2,1,0:T(8,128)(2,1)}), bf16[16,16,1536]{2,1,0:T(8,128)(2,1)S(1)}, u32[]{:S(2)}, u32[]{:S(2)}) %all-to-all-start) | async-done | bytes 786464 | tf_op jit(solution)/shard_map/all_to_all | solution.py:501
  30.9 0.0 copy-done.1
  30.9 1.7 %solve.1 = bf16[16,48,512]{2,1,0:T(8,128)(2,1)S(1)} custom-call(bf16[256,1536]{1,0:T(8,128)(2,1)S(1)} %bitcast.6, bf16[4,768,256]{2,1,0:T(8,128)(2,1)S(1)} %select_ops.1.ops, bf16[64,1536]{1,0:T(8,128)(2,1)S(1)} %select_jac.1.box, bf16[512,768]{1,0:T(8,128)(2,1)S(1)} %copy-done.1), custom_call_target="tpu_custom_call" | custom-call | flops 3000000000 | bytes 5000000 | tf_op jit(solution)/shard_map/solve/pallas_call | solution.py:438
  32.6 16.6 %all_to_all.10.recv = bf16[16,48,512]{2,1,0:T(8,128)(2,1)S(1)} all-to-all(bf16[16,48,512]{2,1,0:T(8,128)(2,1)S(1)} %solve.1), channel_id=1, replica_groups=mesh['tm'=16,'space'=8] {'tm'}, dimensions={0} | all-to-all | bytes 1572864 | tf_op jit(solution)/shard_map/all_to_all | solution.py:506
  49.1 1.2 %unpack.1 = (f32[16,8192]{1,0:T(8,128)}, f32[16,8192]{1,0:T(8,128)}, f32[16,8192]{1,0:T(8,128)}) custom-call(bf16[16,48,512]{2,1,0:T(8,128)(2,1)S(1)} %all_to_all.10.recv), custom_call_target="tpu_custom_call" | custom-call | flops 1000000 | bytes 3000000 | tf_op jit(solution)/shard_map/unpack/pallas_call | solution.py:475
Async XLA Ops:
  2.5 5.6 %collective-permute-start = (bf16[8,16,256]{2,1,0:T(8,128)(2,1)S(1)}, bf16[8,16,256]{2,1,0:T(8,128)(2,1)S(1)}, u32[]{:S(2)}, u32[]{:S(2)}) collective-permute-start(bf16[8,16,256]{2,1,0:T(8,128)(2,1)S(1)} %get-tuple-element.14), channel_id=1, source_target_pairs={{1,2},{3,4},{5,6},{2,1},{4,3},{6,5},{9,10},{11,12},{13,14},{10,9},... | collective-permute-start | bytes 196616 | tf_op jit(solution)/shard_map/ppermute | solution.py:495
  4.4 3.7 %collective-permute-start.1 = (bf16[8,16,256]{2,1,0:T(8,128)(2,1)S(1)}, bf16[8,16,256]{2,1,0:T(8,128)(2,1)S(1)}, u32[]{:S(2)}, u32[]{:S(2)}) collective-permute-start(bf16[8,16,256]{2,1,0:T(8,128)(2,1)S(1)} %get-tuple-element.15), channel_id=1, source_target_pairs={{0,1},{2,3},{4,5},{6,7},{1,0},{3,2},{5,4},{7,6},{8,9},{10,11},{12,... | collective-permute-start | bytes 196616 | tf_op jit(solution)/shard_map/ppermute | solution.py:496
  8.7 22.1 %all-to-all-start = ((bf16[16,16,1536]{2,1,0:T(8,128)(2,1)}), bf16[16,16,1536]{2,1,0:T(8,128)(2,1)S(1)}, u32[]{:S(2)}, u32[]{:S(2)}) async-start(bf16[16,16,1536]{2,1,0:T(8,128)(2,1)} %patch.1), calls=%async_computation | async-start | bytes 1572864 | tf_op jit(solution)/shard_map/all_to_all | solution.py:501
  15.8 8.7 %copy-start = (bf16[128,64,64]{0,2,1:T(8,128)(2,1)S(1)}, bf16[128,64,64]{0,2,1:T(8,128)(2,1)}, u32[]{:S(2)}) copy-start(bf16[128,64,64]{0,2,1:T(8,128)(2,1)} %param.8) | copy-start | bytes 3145732
  15.8 15.1 %copy-start.1 = (bf16[512,768]{1,0:T(8,128)(2,1)S(1)}, bf16[512,768]{1,0:T(8,128)(2,1)}, u32[]{:S(2)}) copy-start(bf16[512,768]{1,0:T(8,128)(2,1)} %constant.2.clone.table) | copy-start | bytes 2359300

commit v6 on v5

--- a/solution.py
+++ b/solution.py
@@ -209,7 +209,7 @@
     for c in range(BS // CHUNK):
         cut = pl.ds(c * CHUNK, CHUNK)
         copies.append(pltpu.make_async_copy(jac.at[cut], local.at[cut], sems.at[3 + c]))
-    for which in (0, 1, 3, 4, 5, 6, 2):
+    for which in (3, 4, 5, 6, 0, 1, 2):
         copies[which].start()
     scale = scales()
     slot = slots_of()
@@ -446,21 +446,21 @@
 
 def unpack_kernel(recv, real, imag, in_time, ready, sems):
     copies = []
-    for zg in range(4):
+    for z in range(LAYERS):
+        zg, d = z // 2, z % 2
         for which, out in enumerate((real, imag, in_time)):
-            for d in range(2):
-                for rest in range(4):
-                    source = 4 * zg + rest
-                    _, yg, xg = box_of(source)
-                    for e in range(2):
-                        at = (2 * zg + d) * LAYER + (2 * yg + e) * ROW + xg * COL
-                        c = 2 * d + e
-                        ready[which, :, at : at + COL] = recv[
-                            source,
-                            which * STEPS : (which + 1) * STEPS,
-                            c * COL : (c + 1) * COL,
-                        ].astype(f32)
-            cut = pl.ds(2 * zg * LAYER, 2 * LAYER)
+            for rest in range(4):
+                source = 4 * zg + rest
+                _, yg, xg = box_of(source)
+                for e in range(2):
+                    at = z * LAYER + (2 * yg + e) * ROW + xg * COL
+                    c = 2 * d + e
+                    ready[which, :, at : at + COL] = recv[
+                        source,
+                        which * STEPS : (which + 1) * STEPS,
+                        c * COL : (c + 1) * COL,
+                    ].astype(f32)
+            cut = pl.ds(z * LAYER, LAYER)
             copy = pltpu.make_async_copy(
                 ready.at[which, :, cut], out.at[:, cut], sems.at[len(copies)]
             )
@@ -476,7 +476,7 @@
         unpack_kernel,
         out_shape=(out, out, out),
         out_specs=(pl.BlockSpec(memory_space=pltpu.HBM),) * 3,
-        scratch_shapes=[pltpu.VMEM((3, STEPS, SLAB), f32), pltpu.SemaphoreType.DMA((12,))],
+        scratch_shapes=[pltpu.VMEM((3, STEPS, SLAB), f32), pltpu.SemaphoreType.DMA((24,))],
         name="unpack",
         compiler_params=pltpu.CompilerParams(vmem_limit_bytes=6 * 2**20),
         cost_estimate=cost(10**6, 3 * 10**6),

time: 51.3 us -> 51.3 us (level)
  no operation moved by 1% of the time
where the time goes in v6:
time: 51.3 us; the launch traced here: 50.4 us
  Pallas kernels  16.8 us (33%)
  blocking collectives  16.6 us (32%)
  starting transfers between devices  11.1 us (22%)
  waiting for transfers between devices  5.28 us (10%)
  between operations  0.71 us (1%)
    all_to_all x1, blocking collectives, per_device(): back = lax.all_to_all(sent, 'tm', 0, 0)  16.6 us
    pallas_call x1, Pallas kernels, select_ops(): pl.pallas_call(ops_kernel, grid=(BS // CHUNK,), in_specs=[spec, spec], ou...  8.66 us
    all_to_all x1, starting transfers between devices, per_device(): recv = lax.all_to_all(packed, 'tm', 0, 0).reshape(LENGTH, BOX)  7.05 us
    all_to_all x1, waiting for transfers between devices, per_device(): recv = lax.all_to_all(packed, 'tm', 0, 0).reshape(LENGTH, BOX)  4.75 us
    ppermute x1, starting transfers between devices, per_device(): near = lax.ppermute(near, 'space', within)  2.1 us
    ppermute x1, starting transfers between devices, per_device(): far = lax.ppermute(far, 'space', across)  1.92 us
    pallas_call x1, Pallas kernels, edges(): pl.pallas_call(edge_kernel, in_specs=[hbm, hbm], out_shape=(edge, edge, j...  1.81 us
    pallas_call x1, Pallas kernels, solve(): pl.pallas_call(solve_kernel, out_shape=jax.ShapeDtypeStruct((PARTS, 3 * S...  1.68 us
  transfers between devices with their start and end apart: 3, of which 2 were waited for; matrix products, arithmetic and copies ran while one was open for 0% of the time, Pallas kernels for 22%

profile of v6, /device:TPU:32, one launch (start us, length us, event | category | flops | bytes accessed | tf_op | source)
XLA Modules:
  0.0 50.4 jit_solution(7440237235716647158)
XLA Ops:
  0.6 1.8 %edges.1 = (bf16[8,16,256]{2,1,0:T(8,128)(2,1)S(1)}, bf16[8,16,256]{2,1,0:T(8,128)(2,1)S(1)}, f32[16,8192]{1,0:T(8,128)S(1)}) custom-call(f32[16,8192]{1,0:T(8,128)} %forcing.1, bf16[64,64,128]{2,1,0:T(8,128)(2,1)} %bitcast.4), custom_call_target="tpu_custom_call" | custom-call | flops 100000000 | bytes 2000000 | tf_op jit(solution)/shard_map/edges/pallas_call | solution.py:246
  2.5 1.9 %collective-permute-start = (bf16[8,16,256]{2,1,0:T(8,128)(2,1)S(1)}, bf16[8,16,256]{2,1,0:T(8,128)(2,1)S(1)}, u32[]{:S(2)}, u32[]{:S(2)}) collective-permute-start(bf16[8,16,256]{2,1,0:T(8,128)(2,1)S(1)} %get-tuple-element.14), channel_id=1, source_target_pairs={{1,2},{3,4},{5,6},{2,1},{4,3},{6,5},{9,10},{11,12},{13,14},{10,9},... | collective-permute-start | bytes 196616 | tf_op jit(solution)/shard_map/ppermute | solution.py:495
  4.4 2.1 %collective-permute-start.1 = (bf16[8,16,256]{2,1,0:T(8,128)(2,1)S(1)}, bf16[8,16,256]{2,1,0:T(8,128)(2,1)S(1)}, u32[]{:S(2)}, u32[]{:S(2)}) collective-permute-start(bf16[8,16,256]{2,1,0:T(8,128)(2,1)S(1)} %get-tuple-element.15), channel_id=1, source_target_pairs={{0,1},{2,3},{4,5},{6,7},{1,0},{3,2},{5,4},{7,6},{8,9},{10,11},{12,... | collective-permute-start | bytes 196616 | tf_op jit(solution)/shard_map/ppermute | solution.py:496
  6.5 1.0 %pack.1.packed = bf16[16,16,1536]{2,1,0:T(8,128)(2,1)} custom-call(f32[16,8192]{1,0:T(8,128)S(1)} %get-tuple-element.16.forcing), custom_call_target="tpu_custom_call" | custom-call | flops 1000000 | bytes 4000000 | tf_op jit(solution)/shard_map/pack/pallas_call | solution.py:102
  7.5 0.5 %collective-permute-done.far = bf16[8,16,256]{2,1,0:T(8,128)(2,1)S(1)} collective-permute-done((bf16[8,16,256]{2,1,0:T(8,128)(2,1)S(1)}, bf16[8,16,256]{2,1,0:T(8,128)(2,1)S(1)}, u32[]{:S(2)}, u32[]{:S(2)}) %collective-permute-start) | collective-permute-done | bytes 65568 | tf_op jit(solution)/shard_map/ppermute | solution.py:495
  8.0 0.0 collective-permute-done.1.near
  8.0 0.6 %patch.1 = bf16[16,16,1536]{2,1,0:T(8,128)(2,1)} custom-call(bf16[16,16,1536]{2,1,0:T(8,128)(2,1)} %pack.1.packed, bf16[8,16,256]{2,1,0:T(8,128)(2,1)S(1)} %collective-permute-done.far, bf16[8,16,256]{2,1,0:T(8,128)(2,1)S(1)} %collective-permute-done.1.near), custom_call_target="tpu_custom_call", output_to_operand_aliasing={{}: (0, {})} | custom-call | flops 1000 | bytes 200000 | tf_op jit(solution)/shard_map/patch/pallas_call | solution.py:142
  8.7 7.0 %all-to-all-start = ((bf16[16,16,1536]{2,1,0:T(8,128)(2,1)}), bf16[16,16,1536]{2,1,0:T(8,128)(2,1)S(1)}, u32[]{:S(2)}, u32[]{:S(2)}) async-start(bf16[16,16,1536]{2,1,0:T(8,128)(2,1)} %patch.1), calls=%async_computation | async-start | bytes 1572864 | tf_op jit(solution)/shard_map/all_to_all | solution.py:501
  15.7 0.0 copy-start
  15.7 0.0 copy-start.1
  15.8 8.7 %select_ops.1.ops = bf16[4,768,256]{2,1,0:T(8,128)(2,1)S(1)} custom-call(bf16[64,448,128]{2,1,0:T(8,128)(2,1)} %bitcast.7, bf16[64,448,128]{2,1,0:T(8,128)(2,1)} %bitcast.8), custom_call_target="tpu_custom_call" | custom-call | flops 4000000000 | bytes 16000000 | tf_op jit(solution)/shard_map/select_ops/pallas_call | solution.py:366
  24.4 0.0 copy-done
  24.4 1.6 %select_jac.1.box = bf16[64,1536]{1,0:T(8,128)(2,1)S(1)} custom-call(bf16[64,64,128]{2,1,0:T(8,128)(2,1)S(1)} %bitcast.5, bf16[8,16,256]{2,1,0:T(8,128)(2,1)S(1)} %collective-permute-done.far, bf16[8,16,256]{2,1,0:T(8,128)(2,1)S(1)} %collective-permute-done.1.near), custom_call_target="tpu_custom_call" | custom-call | flops 1000000000 | bytes 2000000 | tf_op jit(solution)/shard_map/select_jac/pallas_call | solution.py:297
  26.1 4.8 %all-to-all-done = bf16[16,16,1536]{2,1,0:T(8,128)(2,1)S(1)} async-done(((bf16[16,16,1536]{2,1,0:T(8,128)(2,1)}), bf16[16,16,1536]{2,1,0:T(8,128)(2,1)S(1)}, u32[]{:S(2)}, u32[]{:S(2)}) %all-to-all-start) | async-done | bytes 786464 | tf_op jit(solution)/shard_map/all_to_all | solution.py:501
  30.8 0.0 copy-done.1
  30.8 1.7 %solve.1 = bf16[16,48,512]{2,1,0:T(8,128)(2,1)S(1)} custom-call(bf16[256,1536]{1,0:T(8,128)(2,1)S(1)} %bitcast.6, bf16[4,768,256]{2,1,0:T(8,128)(2,1)S(1)} %select_ops.1.ops, bf16[64,1536]{1,0:T(8,128)(2,1)S(1)} %select_jac.1.box, bf16[512,768]{1,0:T(8,128)(2,1)S(1)} %copy-done.1), custom_call_target="tpu_custom_call" | custom-call | flops 3000000000 | bytes 5000000 | tf_op jit(solution)/shard_map/solve/pallas_call | solution.py:438
  32.5 16.6 %all_to_all.10.recv = bf16[16,48,512]{2,1,0:T(8,128)(2,1)S(1)} all-to-all(bf16[16,48,512]{2,1,0:T(8,128)(2,1)S(1)} %solve.1), channel_id=1, replica_groups=mesh['tm'=16,'space'=8] {'tm'}, dimensions={0} | all-to-all | bytes 1572864 | tf_op jit(solution)/shard_map/all_to_all | solution.py:506
  49.1 1.3 %unpack.1 = (f32[16,8192]{1,0:T(8,128)}, f32[16,8192]{1,0:T(8,128)}, f32[16,8192]{1,0:T(8,128)}) custom-call(bf16[16,48,512]{2,1,0:T(8,128)(2,1)S(1)} %all_to_all.10.recv), custom_call_target="tpu_custom_call" | custom-call | flops 1000000 | bytes 3000000 | tf_op jit(solution)/shard_map/unpack/pallas_call | solution.py:475
Async XLA Ops:
  2.5 5.6 %collective-permute-start = (bf16[8,16,256]{2,1,0:T(8,128)(2,1)S(1)}, bf16[8,16,256]{2,1,0:T(8,128)(2,1)S(1)}, u32[]{:S(2)}, u32[]{:S(2)}) collective-permute-start(bf16[8,16,256]{2,1,0:T(8,128)(2,1)S(1)} %get-tuple-element.14), channel_id=1, source_target_pairs={{1,2},{3,4},{5,6},{2,1},{4,3},{6,5},{9,10},{11,12},{13,14},{10,9},... | collective-permute-start | bytes 196616 | tf_op jit(solution)/shard_map/ppermute | solution.py:495
  4.4 3.7 %collective-permute-start.1 = (bf16[8,16,256]{2,1,0:T(8,128)(2,1)S(1)}, bf16[8,16,256]{2,1,0:T(8,128)(2,1)S(1)}, u32[]{:S(2)}, u32[]{:S(2)}) collective-permute-start(bf16[8,16,256]{2,1,0:T(8,128)(2,1)S(1)} %get-tuple-element.15), channel_id=1, source_target_pairs={{0,1},{2,3},{4,5},{6,7},{1,0},{3,2},{5,4},{7,6},{8,9},{10,11},{12,... | collective-permute-start | bytes 196616 | tf_op jit(solution)/shard_map/ppermute | solution.py:496
  8.7 22.1 %all-to-all-start = ((bf16[16,16,1536]{2,1,0:T(8,128)(2,1)}), bf16[16,16,1536]{2,1,0:T(8,128)(2,1)S(1)}, u32[]{:S(2)}, u32[]{:S(2)}) async-start(bf16[16,16,1536]{2,1,0:T(8,128)(2,1)} %patch.1), calls=%async_computation | async-start | bytes 1572864 | tf_op jit(solution)/shard_map/all_to_all | solution.py:501
  15.7 8.7 %copy-start = (bf16[128,64,64]{0,2,1:T(8,128)(2,1)S(1)}, bf16[128,64,64]{0,2,1:T(8,128)(2,1)}, u32[]{:S(2)}) copy-start(bf16[128,64,64]{0,2,1:T(8,128)(2,1)} %param.8) | copy-start | bytes 3145732
  15.7 15.1 %copy-start.1 = (bf16[512,768]{1,0:T(8,128)(2,1)S(1)}, bf16[512,768]{1,0:T(8,128)(2,1)}, u32[]{:S(2)}) copy-start(bf16[512,768]{1,0:T(8,128)(2,1)} %constant.2.clone.table) | copy-start | bytes 2359300

commit v7 on v6

--- a/solution.py
+++ b/solution.py
@@ -397,8 +397,6 @@
     halves += [dot(fields(2 * p, 2), diagonals[p]).astype(bf16) for p in range(2, 6)]
     lows = [half[:, e * COL : (e + 1) * COL] for half in halves for e in range(2)]
 
-    ids = step_ids(0, LENGTH, 2 * COL).astype(f32)
-    growth = jnp.exp(ids * -LOG_STEP)
     seconds = []
     for dz in range(2):
         residues = []
@@ -420,7 +418,7 @@
             residue = fields(pair, 1).astype(f32) - image[:, :COL] + MODULUS * earlier
             residues.append(residue.astype(bf16))
         second = firsts[dz] + dot(jnp.concatenate(residues, axis=1), diagonals[dz])
-        in_time = (second * growth).astype(bf16)
+        in_time = second.astype(bf16)
         for dest in range(PARTS):
             out[dest, 2 * STEPS :, 2 * dz * COL : 2 * (dz + 1) * COL] = in_time[
                 dest * STEPS : (dest + 1) * STEPS
@@ -445,6 +443,8 @@
 
 
 def unpack_kernel(recv, real, imag, in_time, ready, sems):
+    ids = step_ids(lax.axis_index("tm"), STEPS, COL).astype(f32)
+    growth = jnp.exp(ids * -LOG_STEP)
     copies = []
     for z in range(LAYERS):
         zg, d = z // 2, z % 2
@@ -455,11 +455,14 @@
                 for e in range(2):
                     at = z * LAYER + (2 * yg + e) * ROW + xg * COL
                     c = 2 * d + e
-                    ready[which, :, at : at + COL] = recv[
+                    value = recv[
                         source,
                         which * STEPS : (which + 1) * STEPS,
                         c * COL : (c + 1) * COL,
                     ].astype(f32)
+                    ready[which, :, at : at + COL] = (
+                        value * growth if which == 2 else value
+                    )
             cut = pl.ds(z * LAYER, LAYER)
             copy = pltpu.make_async_copy(
                 ready.at[which, :, cut], out.at[:, cut], sems.at[len(copies)]

time: 51.3 us -> 51.3 us (level)
  no operation moved by 1% of the time
where the time goes in v7:
time: 51.3 us; the launch traced here: 50.4 us
  Pallas kernels  16.8 us (33%)
  blocking collectives  16.6 us (32%)
  starting transfers between devices  11.1 us (22%)
  waiting for transfers between devices  5.28 us (10%)
  between operations  0.71 us (1%)
    all_to_all x1, blocking collectives, per_device(): back = lax.all_to_all(sent, 'tm', 0, 0)  16.6 us
    pallas_call x1, Pallas kernels, select_ops(): pl.pallas_call(ops_kernel, grid=(BS // CHUNK,), in_specs=[spec, spec], ou...  8.66 us
    all_to_all x1, starting transfers between devices, per_device(): recv = lax.all_to_all(packed, 'tm', 0, 0).reshape(LENGTH, BOX)  7.05 us
    all_to_all x1, waiting for transfers between devices, per_device(): recv = lax.all_to_all(packed, 'tm', 0, 0).reshape(LENGTH, BOX)  4.75 us
    ppermute x1, starting transfers between devices, per_device(): near = lax.ppermute(near, 'space', within)  2.1 us
    ppermute x1, starting transfers between devices, per_device(): far = lax.ppermute(far, 'space', across)  1.92 us
    pallas_call x1, Pallas kernels, edges(): pl.pallas_call(edge_kernel, in_specs=[hbm, hbm], out_shape=(edge, edge, j...  1.81 us
    pallas_call x1, Pallas kernels, solve(): pl.pallas_call(solve_kernel, out_shape=jax.ShapeDtypeStruct((PARTS, 3 * S...  1.68 us
  transfers between devices with their start and end apart: 3, of which 2 were waited for; matrix products, arithmetic and copies ran while one was open for 0% of the time, Pallas kernels for 22%

profile of v7, /device:TPU:32, one launch (start us, length us, event | category | flops | bytes accessed | tf_op | source)
XLA Modules:
  0.0 50.4 jit_solution(14150470220741679918)
XLA Ops:
  0.6 1.8 %edges.1 = (bf16[8,16,256]{2,1,0:T(8,128)(2,1)S(1)}, bf16[8,16,256]{2,1,0:T(8,128)(2,1)S(1)}, f32[16,8192]{1,0:T(8,128)S(1)}) custom-call(f32[16,8192]{1,0:T(8,128)} %forcing.1, bf16[64,64,128]{2,1,0:T(8,128)(2,1)} %bitcast.4), custom_call_target="tpu_custom_call" | custom-call | flops 100000000 | bytes 2000000 | tf_op jit(solution)/shard_map/edges/pallas_call | solution.py:246
  2.5 1.9 %collective-permute-start = (bf16[8,16,256]{2,1,0:T(8,128)(2,1)S(1)}, bf16[8,16,256]{2,1,0:T(8,128)(2,1)S(1)}, u32[]{:S(2)}, u32[]{:S(2)}) collective-permute-start(bf16[8,16,256]{2,1,0:T(8,128)(2,1)S(1)} %get-tuple-element.14), channel_id=1, source_target_pairs={{1,2},{3,4},{5,6},{2,1},{4,3},{6,5},{9,10},{11,12},{13,14},{10,9},... | collective-permute-start | bytes 196616 | tf_op jit(solution)/shard_map/ppermute | solution.py:498
  4.4 2.1 %collective-permute-start.1 = (bf16[8,16,256]{2,1,0:T(8,128)(2,1)S(1)}, bf16[8,16,256]{2,1,0:T(8,128)(2,1)S(1)}, u32[]{:S(2)}, u32[]{:S(2)}) collective-permute-start(bf16[8,16,256]{2,1,0:T(8,128)(2,1)S(1)} %get-tuple-element.15), channel_id=1, source_target_pairs={{0,1},{2,3},{4,5},{6,7},{1,0},{3,2},{5,4},{7,6},{8,9},{10,11},{12,... | collective-permute-start | bytes 196616 | tf_op jit(solution)/shard_map/ppermute | solution.py:499
  6.5 1.0 %pack.1.packed = bf16[16,16,1536]{2,1,0:T(8,128)(2,1)} custom-call(f32[16,8192]{1,0:T(8,128)S(1)} %get-tuple-element.16.forcing), custom_call_target="tpu_custom_call" | custom-call | flops 1000000 | bytes 4000000 | tf_op jit(solution)/shard_map/pack/pallas_call | solution.py:102
  7.5 0.5 %collective-permute-done.far = bf16[8,16,256]{2,1,0:T(8,128)(2,1)S(1)} collective-permute-done((bf16[8,16,256]{2,1,0:T(8,128)(2,1)S(1)}, bf16[8,16,256]{2,1,0:T(8,128)(2,1)S(1)}, u32[]{:S(2)}, u32[]{:S(2)}) %collective-permute-start) | collective-permute-done | bytes 65568 | tf_op jit(solution)/shard_map/ppermute | solution.py:498
  8.0 0.0 collective-permute-done.1.near
  8.0 0.6 %patch.1 = bf16[16,16,1536]{2,1,0:T(8,128)(2,1)} custom-call(bf16[16,16,1536]{2,1,0:T(8,128)(2,1)} %pack.1.packed, bf16[8,16,256]{2,1,0:T(8,128)(2,1)S(1)} %collective-permute-done.far, bf16[8,16,256]{2,1,0:T(8,128)(2,1)S(1)} %collective-permute-done.1.near), custom_call_target="tpu_custom_call", output_to_operand_aliasing={{}: (0, {})} | custom-call | flops 1000 | bytes 200000 | tf_op jit(solution)/shard_map/patch/pallas_call | solution.py:142
  8.7 7.0 %all-to-all-start = ((bf16[16,16,1536]{2,1,0:T(8,128)(2,1)}), bf16[16,16,1536]{2,1,0:T(8,128)(2,1)S(1)}, u32[]{:S(2)}, u32[]{:S(2)}) async-start(bf16[16,16,1536]{2,1,0:T(8,128)(2,1)} %patch.1), calls=%async_computation | async-start | bytes 1572864 | tf_op jit(solution)/shard_map/all_to_all | solution.py:504
  15.7 0.0 copy-start
  15.7 0.0 copy-start.1
  15.8 8.7 %select_ops.1.ops = bf16[4,768,256]{2,1,0:T(8,128)(2,1)S(1)} custom-call(bf16[64,448,128]{2,1,0:T(8,128)(2,1)} %bitcast.7, bf16[64,448,128]{2,1,0:T(8,128)(2,1)} %bitcast.8), custom_call_target="tpu_custom_call" | custom-call | flops 4000000000 | bytes 16000000 | tf_op jit(solution)/shard_map/select_ops/pallas_call | solution.py:366
  24.4 0.0 copy-done
  24.4 1.6 %select_jac.1.box = bf16[64,1536]{1,0:T(8,128)(2,1)S(1)} custom-call(bf16[64,64,128]{2,1,0:T(8,128)(2,1)S(1)} %bitcast.5, bf16[8,16,256]{2,1,0:T(8,128)(2,1)S(1)} %collective-permute-done.far, bf16[8,16,256]{2,1,0:T(8,128)(2,1)S(1)} %collective-permute-done.1.near), custom_call_target="tpu_custom_call" | custom-call | flops 1000000000 | bytes 2000000 | tf_op jit(solution)/shard_map/select_jac/pallas_call | solution.py:297
  26.1 4.8 %all-to-all-done = bf16[16,16,1536]{2,1,0:T(8,128)(2,1)S(1)} async-done(((bf16[16,16,1536]{2,1,0:T(8,128)(2,1)}), bf16[16,16,1536]{2,1,0:T(8,128)(2,1)S(1)}, u32[]{:S(2)}, u32[]{:S(2)}) %all-to-all-start) | async-done | bytes 786464 | tf_op jit(solution)/shard_map/all_to_all | solution.py:504
  30.8 0.0 copy-done.1
  30.8 1.7 %solve.1 = bf16[16,48,512]{2,1,0:T(8,128)(2,1)S(1)} custom-call(bf16[256,1536]{1,0:T(8,128)(2,1)S(1)} %bitcast.6, bf16[4,768,256]{2,1,0:T(8,128)(2,1)S(1)} %select_ops.1.ops, bf16[64,1536]{1,0:T(8,128)(2,1)S(1)} %select_jac.1.box, bf16[512,768]{1,0:T(8,128)(2,1)S(1)} %copy-done.1), custom_call_target="tpu_custom_call" | custom-call | flops 3000000000 | bytes 5000000 | tf_op jit(solution)/shard_map/solve/pallas_call | solution.py:436
  32.5 16.6 %all_to_all.10.recv = bf16[16,48,512]{2,1,0:T(8,128)(2,1)S(1)} all-to-all(bf16[16,48,512]{2,1,0:T(8,128)(2,1)S(1)} %solve.1), channel_id=1, replica_groups=mesh['tm'=16,'space'=8] {'tm'}, dimensions={0} | all-to-all | bytes 1572864 | tf_op jit(solution)/shard_map/all_to_all | solution.py:509
  49.1 1.3 %unpack.1 = (f32[16,8192]{1,0:T(8,128)}, f32[16,8192]{1,0:T(8,128)}, f32[16,8192]{1,0:T(8,128)}) custom-call(bf16[16,48,512]{2,1,0:T(8,128)(2,1)S(1)} %all_to_all.10.recv), custom_call_target="tpu_custom_call" | custom-call | flops 1000000 | bytes 3000000 | tf_op jit(solution)/shard_map/unpack/pallas_call | solution.py:478
Async XLA Ops:
  2.5 5.6 %collective-permute-start = (bf16[8,16,256]{2,1,0:T(8,128)(2,1)S(1)}, bf16[8,16,256]{2,1,0:T(8,128)(2,1)S(1)}, u32[]{:S(2)}, u32[]{:S(2)}) collective-permute-start(bf16[8,16,256]{2,1,0:T(8,128)(2,1)S(1)} %get-tuple-element.14), channel_id=1, source_target_pairs={{1,2},{3,4},{5,6},{2,1},{4,3},{6,5},{9,10},{11,12},{13,14},{10,9},... | collective-permute-start | bytes 196616 | tf_op jit(solution)/shard_map/ppermute | solution.py:498
  4.4 3.7 %collective-permute-start.1 = (bf16[8,16,256]{2,1,0:T(8,128)(2,1)S(1)}, bf16[8,16,256]{2,1,0:T(8,128)(2,1)S(1)}, u32[]{:S(2)}, u32[]{:S(2)}) collective-permute-start(bf16[8,16,256]{2,1,0:T(8,128)(2,1)S(1)} %get-tuple-element.15), channel_id=1, source_target_pairs={{0,1},{2,3},{4,5},{6,7},{1,0},{3,2},{5,4},{7,6},{8,9},{10,11},{12,... | collective-permute-start | bytes 196616 | tf_op jit(solution)/shard_map/ppermute | solution.py:499
  8.7 22.1 %all-to-all-start = ((bf16[16,16,1536]{2,1,0:T(8,128)(2,1)}), bf16[16,16,1536]{2,1,0:T(8,128)(2,1)S(1)}, u32[]{:S(2)}, u32[]{:S(2)}) async-start(bf16[16,16,1536]{2,1,0:T(8,128)(2,1)} %patch.1), calls=%async_computation | async-start | bytes 1572864 | tf_op jit(solution)/shard_map/all_to_all | solution.py:504
  15.7 8.7 %copy-start = (bf16[128,64,64]{0,2,1:T(8,128)(2,1)S(1)}, bf16[128,64,64]{0,2,1:T(8,128)(2,1)}, u32[]{:S(2)}) copy-start(bf16[128,64,64]{0,2,1:T(8,128)(2,1)} %param.8) | copy-start | bytes 3145732
  15.7 15.1 %copy-start.1 = (bf16[512,768]{1,0:T(8,128)(2,1)S(1)}, bf16[512,768]{1,0:T(8,128)(2,1)}, u32[]{:S(2)}) copy-start(bf16[512,768]{1,0:T(8,128)(2,1)} %constant.2.clone.table) | copy-start | bytes 2359300
